TPU v7x, 256 devices: a whole 4x4x8 slice. The times are simulated.
256 devices in a mesh: tm: 4 (over y_lo, core), pts: 64 (over y_hi, z, x).
Axes of the slice: x: 4, y: 4 (y_hi: 2, y_lo: 2; y = y_hi * 2 + y_lo), z: 8, core: 2. Of those that a mesh axis runs over, the one named last changes fastest.
Arguments:
- saved_paths: bfloat16 [4096, 64, 512], P('tm', 'pts')
- pca_basis: bfloat16 [4096, 4096], P('pts', 'tm')
- vol_surface: float32 [4096, 512], P('tm'), may hold values from 0.5 to 2
- chol_factor: bfloat16 [512, 512], replicated
- exposure_load: float32 [32, 512], replicated, may hold values from -0.25 to 0.25
- reset_load: float32 [32, 512], replicated, may hold values from -0.0234375 to 0.0234375
- strikes: float32 [32], replicated, may hold values from -4 to 4
- bucket_weight: float32 [32], replicated, may hold values from 0.5 to 2
- bucket_start: int32 [32], replicated, may hold values from 0 to 4095, as said below
- generator: int32 [512], replicated, may hold values from 1 to 1048575
- point_ids: int32 [64], P('pts'), may hold values from 0 to 1048575
Outputs:
- normal_adjoint: float32 [4096, 64, 512], P('tm', 'pts')
- vol_greeks: float32 [4096, 512], P('tm')
- chol_greeks: float32 [512, 512], replicated
Inputs may be any that keep to these rules, and one draw needn't show every extreme that they name: bucket_start[0] = 0, the last entry is 4095, and the entries rise strictly.
All inputs are finite; a program needn't handle non-finite values.
Results may differ from a plain program's by a relative error of at most 0.0042.
Values may be sent and summed in bfloat16 or wider, within the bound.
No kernel may reach another device: no remote copies, remote signals or barrier semaphores. Data moves between devices by JAX's collectives and lax.ppermute only.
A program may use at most 128 MiB of HBM per device.

v0:
```python
import jax
import jax.numpy as jnp
from jax import lax
from jax.experimental import pallas as pl
from jax.experimental.pallas import tpu as pltpu
from jax.sharding import Mesh, PartitionSpec as P

BF = jnp.bfloat16
F32 = jnp.float32
I32 = jnp.int32
ALL = ("yl", "c", "yh", "z", "x1", "x0")
TM = ("yl", "c")
X = ("x1", "x0")
PTS = ("yh", "z", "x1", "x0")
PEERS = ("yh", "x0")
NB = 32
STEPS = 1024
BLOCKS = 4
CHUNK = 256
NF = 512
GROUP = 4
ROWS = STEPS // GROUP
WROWS = 5 * NB
MIB = 1024 * 1024

NN = (((1,), (0,)), ((), ()))
NT = (((1,), (1,)), ((), ()))
TN = (((0,), (0,)), ((), ()))


def dot(a, b, dims):
    return lax.dot_general(a, b, dims, preferred_element_type=F32)


def split2(x):
    hi = x.astype(BF)
    return hi, (x - hi.astype(F32)).astype(BF)


def split3(x):
    hi, mid = split2(x)
    return hi, mid, (x - hi.astype(F32) - mid.astype(F32)).astype(BF)


def column(row, shift=0):
    i = lax.broadcasted_iota(I32, (NB, NB), 0)
    j = lax.broadcasted_iota(I32, (NB, NB), 1)
    return jnp.sum(jnp.where(j == i + shift, row, 0), axis=1, keepdims=True)


def bucket_ends(bstart):
    start = column(bstart)
    last = lax.broadcasted_iota(I32, (NB, 1), 0) == NB - 1
    return start, jnp.where(last, BLOCKS * STEPS, column(bstart, 1))


def bucket_rows(bstart):
    i = lax.broadcasted_iota(I32, (NB, NB), 0)
    j = lax.broadcasted_iota(I32, (NB, NB), 1)
    nxt = jnp.sum(jnp.where(i == j + 1, column(bstart), 0), axis=0, keepdims=True)
    last = lax.broadcasted_iota(I32, (1, NB), 1) == NB - 1
    nxt = jnp.where(last, BLOCKS * STEPS, nxt)
    return jnp.concatenate([bstart] * 4, axis=1), jnp.concatenate([nxt] * 4, axis=1)


def one_hots(first_step, count, start, nxt):
    t = first_step + lax.broadcasted_iota(I32, (NB, count), 1)
    member = jnp.where((t >= start) & (t < nxt), 1.0, 0.0)
    at_start = jnp.where(t == start, 1.0, 0.0)
    return member, at_start


def own_block():
    return lax.axis_index("yl") * 2 + lax.axis_index("c")


def margin_kernel(pid, paths, vol, chol, gen, load, reset, bstart, out):
    i = pl.program_id(0)
    low = (pid[0] * (gen[...] & 1023)) & 1048575
    high = ((pid[0] * (gen[...] >> 10)) & 1023) << 10
    residue = (low + high) & 1048575
    start_state = 0.5 * 3.4641016151377544 * ((residue.astype(F32) + 0.5) / 1048576.0 - 0.5)
    state = start_state + vol[...] * dot(paths[...], chol[...], NT)
    s1, s2 = split2(state)
    l1, l2 = split2(load[...])
    r1, r2 = split2(reset[...])
    none = jnp.zeros_like(l1)
    by_bucket = dot(s1, jnp.concatenate([l1, l2, r1, r2], axis=0), NT) + dot(
        s2, jnp.concatenate([l1, none, r1, none], axis=0), NT
    )
    start, nxt = bucket_rows(bstart[...])
    t = own_block() * STEPS + i * CHUNK + lax.broadcasted_iota(I32, (CHUNK, 4 * NB), 0)
    lane = lax.broadcasted_iota(I32, (CHUNK, 4 * NB), 1)
    margin = jnp.where((lane < 2 * NB) & (t >= start) & (t < nxt), by_bucket, 0.0)
    term = jnp.where((lane >= 2 * NB) & (t == start), by_bucket, 0.0)
    margin = jnp.sum(margin, axis=1, keepdims=True)
    term = jnp.sum(term, axis=1, keepdims=True)
    both = jnp.where(lane == 0, margin, jnp.where(lane == 1, term, 0.0))
    out[...] = jnp.transpose(both)[0:2]


def group_index():
    return lax.axis_index("yh") * 2 + lax.axis_index("x0")


def bucket_values(y, hots, strikes, weight):
    term = sum(jnp.sum(hots[b][1] * y(b)[1:2], axis=1, keepdims=True) for b in range(BLOCKS))
    offset = term - strikes
    total = jnp.zeros((NB, 1), F32)
    rows = []
    for b in range(BLOCKS):
        row = step_sens(y(b), hots[b][0], offset, weight)
        total = total + jnp.sum(hots[b][0] * row, axis=1, keepdims=True)
        rows.append(row)
    return rows, total, offset


def step_sens(y, member, offset, weight):
    margin = y[0:1] + jnp.sum(member * offset, axis=0, keepdims=True)
    gain = jnp.sum(member * weight, axis=0, keepdims=True)
    return gain * jax.nn.sigmoid(margin)


def all_hots(start, nxt):
    return [one_hots(b * STEPS, STEPS, start, nxt) for b in range(BLOCKS)]


def x_index():
    return lax.axis_index("x1") * 2 + lax.axis_index("x0")


def sens_kernel(
    y, paths, vol, chol, load, reset, strikes, weight, bstart, kept, o1, o2, o3, wt, bmat
):
    i = pl.program_id(0)

    @pl.when(i == 0)
    def _():
        start, nxt = bucket_ends(bstart[...])
        w = column(weight[...])
        own = own_block()
        _, total, offset = bucket_values(
            lambda b: y[b], all_hots(start, nxt), column(strikes[...]), w
        )
        member, at_start = one_hots(own * STEPS, STEPS, start, nxt)
        m1, m2 = split2(member * step_sens(y[own], member, offset, w))
        a = at_start.astype(BF)
        wt[...] = jnp.concatenate([m1, m1, m2, a, a], axis=0)
        l1, l2 = split2(load[...])
        r1, r2 = split2(total * reset[...])
        bmat[...] = jnp.concatenate([l1, l2, l1, r1, r2], axis=0)

    at = pl.ds(pl.multiple_of(lax.rem(x_index() + i, 4) * CHUNK, CHUNK), CHUNK)
    term = dot(wt[:, at], bmat[...], TN) * dot(paths[at, :], chol[...], NT)

    @pl.when(i == 0)
    def _():
        kept[...] = term

    for k, o in enumerate((o1, o2, o3)):

        @pl.when(i == k + 1)
        def _(o=o):
            o[...] = term.astype(BF)


def chol_kernel(wt, bmat, paths, vol, kept, sent, acc):
    i = pl.program_id(0)
    at = pl.ds(pl.multiple_of(i * CHUNK, CHUNK), CHUNK)
    scaled = (vol[...] * dot(wt[:, at], bmat[...], TN)).astype(BF)
    new = dot(scaled, paths[...], TN)

    @pl.when(i == 0)
    def _():
        acc[...] = new

    @pl.when(i > 0)
    def _():
        acc[...] += new

    @pl.when(i == STEPS // CHUNK - 1)
    def _():
        c = lax.axis_index("c")
        kept[...] = acc[pl.ds(pl.multiple_of(c * 256, 256), 256), :]
        sent[...] = acc[pl.ds(pl.multiple_of((1 - c) * 256, 256), 256), :]


def chol_split_kernel(own, got, kept, sent):
    yl = lax.axis_index("yl")
    for o, at in ((kept, yl), (sent, 1 - yl)):
        rows = pl.ds(pl.multiple_of(at * 128, 128), 128)
        o[...] = own[rows, :] + got[rows, :]


def sum_x_kernel(kept, g1, g2, g3, c0, c1, out):
    for z in range(8):
        rows = slice(z * 32, z * 32 + 32)
        v = kept[rows, :] + g1[rows, :].astype(F32) + g2[rows, :].astype(F32)
        v = v + g3[rows, :].astype(F32)
        rows = slice(z * 16, z * 16 + 16)
        out[z] = jnp.concatenate([v, c0[rows, :] + c1[rows, :]], axis=0).astype(BF)


def sum_z_kernel(parts, out):
    total = parts[0].astype(F32)
    for k in range(1, parts.shape[0]):
        total = total + parts[k].astype(F32)
    out[...] = total


def total_kernel(own, got, out):
    total = (own[...] + got[...]).astype(BF)
    for z in range(8):
        out[z] = total


def gather_z_kernel(parts, out):
    for z in range(8):
        out[z * 32 : z * 32 + 32, :] = parts[z, 0:32]
        out[256 + z * 16 : 272 + z * 16, :] = parts[z, 32:48]


def greeks_kernel(own, g1, g2, g3, vol_out, chol_out):
    chol = jnp.zeros((128, NF), F32)
    for d, g in enumerate((own, g1, g2, g3)):
        at = pl.ds(pl.multiple_of(lax.rem(x_index() + 4 - d, 4) * 256, 256), 256)
        vol_out[at, :] = g[0:256, :].astype(F32)
        chol = chol + g[256:384, :].astype(F32)
    chol_out[...] = chol.astype(BF)


def chol_half_kernel(own, got, out):
    yl = lax.axis_index("yl")
    for g, at in ((own, yl), (got, 1 - yl)):
        out[pl.ds(pl.multiple_of(at * 128, 128), 128), :] = g[...]


def chol_out_kernel(own, got, out):
    c = lax.axis_index("c")
    for g, at in ((own, c), (got, 1 - c)):
        out[pl.ds(pl.multiple_of(at * 256, 256), 256), :] = g[...].astype(F32) / (BLOCKS * STEPS)


def points_kernel(y, reset, strikes, weight, bstart, cols, radj):
    start, nxt = bucket_ends(bstart[...])
    hots = all_hots(start, nxt)
    w, k = column(weight[...]), column(strikes[...])
    rows = [[] for _ in range(BLOCKS)]
    for q in range(GROUP):
        g = group_index() ^ q
        sens, total, _ = bucket_values(lambda b: y[g, b], hots, k, w)
        radj[q] = total * reset[...]
        for b in range(BLOCKS):
            rows[b].append(sens[b])
    for b in range(BLOCKS):
        cols[b] = jnp.transpose(jnp.concatenate(rows[b] + rows[b], axis=0))


def adjoint_kernel(
    basis_hbm, vol_hbm, s1a, s1b, s2a, s2b, s3a, s3b, cols, radj, chol, load, bstart,
    own, o1, o2, o3, scaled, acc, basis, vol, vols, sems,
):
    half = STEPS // 2
    copies = [[pltpu.make_async_copy(vol_hbm, vol, sems.at[0])]]
    for r, pair in enumerate(((s1a, s1b), (s2a, s2b), (s3a, s3b))):
        copies.append(
            [
                pltpu.make_async_copy(p, vols.at[r, pl.ds(h * half, half)], sems.at[1 + 2 * r + h])
                for h, p in enumerate(pair)
            ]
        )
    for r in range(BLOCKS):
        source = basis_hbm.at[r & 1, r >> 1]
        copies[r].append(pltpu.make_async_copy(source, basis.at[r], sems.at[7 + r]))
        for copy in copies[r]:
            copy.start()
    start, nxt = bucket_ends(bstart[...])
    load_parts = jnp.concatenate(split3(load[...]), axis=0)
    at_resets = jnp.zeros((ROWS, NB), F32)
    vol_resets = jnp.zeros((NB, NF), F32)
    for r in range(BLOCKS):
        for copy in copies[r]:
            copy.wait()
        b = own_block() ^ r
        member, at_start = one_hots(b * STEPS, STEPS, start, nxt)
        member, at_start = member.astype(BF), at_start.astype(BF)
        for j in range(STEPS // CHUNK):
            rows = slice(j * CHUNK, (j + 1) * CHUNK)
            v = vols[r - 1, rows, :] if r else vol[rows, :]
            hot = member[:, rows]
            loads = dot(jnp.concatenate([hot, hot, hot], axis=0), load_parts, TN)
            vol_load = v.astype(F32) * loads
            for q in range(GROUP):
                part = vol_load * cols[b, rows, q : q + 1]
                scaled[r % 2, rows, q * NF : (q + 1) * NF] = part.astype(BF)
            for h in (v,) if r else split2(v):
                vol_resets = vol_resets + dot(at_start[:, rows], h, NN)
        lhs = jnp.concatenate([basis[r, x & 1, x >> 1] for x in range(4)], axis=0)
        new = dot(lhs, scaled[r % 2], NN)
        acc[...] = new if r == 0 else acc[...] + new
        at_resets = at_resets + dot(lhs, at_start, NT)
    at_resets = at_resets.astype(BF)
    for q, o in enumerate((own, o1, o2, o3)):
        more = dot(at_resets, (vol_resets * radj[q]).astype(BF), NN)
        h1, h2 = split2(acc[:, q * NF : (q + 1) * NF] + more)
        o[...] = (dot(h1, chol[...], NN) + dot(h2, chol[...], NN)).astype(o.dtype)


def normals_kernel(own, g1, g2, g3, out):
    for q, g in enumerate((own, g1, g2, g3)):
        first = pl.multiple_of((group_index() ^ q) * (ROWS * 4), ROWS * 4)
        for j in range(4):
            at = pl.ds(first + j, ROWS, stride=4)
            out[at, :] = g[:, j * 128 : (j + 1) * 128].astype(F32)


def full(shape):
    return pl.BlockSpec(shape, lambda *_: (0,) * len(shape))


def call(kernel, args, outs, name, cost, vmem=40, scratch=(), **kw):
    single = len(outs) == 1
    shapes = [jax.ShapeDtypeStruct(s, d) for s, d in outs]
    spec = dict(
        in_specs=[full(a.shape) for a in args], out_specs=[full(s.shape) for s in shapes], grid=(1,)
    )
    spec.update(kw)
    if single and isinstance(spec["out_specs"], list):
        spec["out_specs"] = spec["out_specs"][0]
    return pl.pallas_call(
        kernel,
        out_shape=shapes[0] if single else shapes,
        scratch_shapes=list(scratch),
        cost_estimate=pl.CostEstimate(flops=cost[0], bytes_accessed=cost[1], transcendentals=0),
        compiler_params=pltpu.CompilerParams(vmem_limit_bytes=vmem * MIB),
        name=name,
        **spec,
    )(*args)


def basis_moves(d):
    moves = []
    for yl in range(2):
        for c in range(2):
            for yh in range(2):
                for z in range(8):
                    for x in range(4):
                        src = (((yl * 2 + c) * 2 + yh) * 8 + z) * 4 + x
                        z2, z1, z0 = z >> 2, (z >> 1) & 1, z & 1
                        to_z = (c ^ z2) * 4 + (yl ^ yh) * 2 + (x & 1)
                        to_x = ((x >> 1) ^ d) * 2 + z0
                        moves.append((src, (((yh * 2 + z2) * 2 + z1) * 8 + to_z) * 4 + to_x))
    return moves


def swap(x, axis):
    return lax.ppermute(x, axis, [(0, 1), (1, 0)])


def shift_x(x, d):
    return lax.ppermute(x, X, [(i, (i + d) % 4) for i in range(4)])


def exchange(x, axes):
    return lax.all_to_all(x, axes, split_axis=0, concat_axis=0, tiled=True)


def after(x, *first):
    return lax.optimization_barrier((x,) + first)[0]


def body(
    saved_paths,
    pca_basis,
    vol_surface,
    chol_factor,
    exposure_load,
    reset_load,
    strikes,
    bucket_weight,
    bucket_start,
    generator,
    point_ids,
):
    paths = saved_paths.reshape(STEPS, NF)
    bstart = bucket_start.reshape(1, NB)
    rows = (reset_load, strikes.reshape(1, NB), bucket_weight.reshape(1, NB), bstart)

    moved = [lax.ppermute(pca_basis, ALL, basis_moves(d)) for d in range(2)]
    chunks = STEPS // CHUNK
    row_spec = pl.BlockSpec((CHUNK, NF), lambda i: (i, 0))
    square = full((NF, NF))
    vol_a = vol_surface[: STEPS // 2].astype(BF)
    vol_b = vol_surface[STEPS // 2 :].astype(BF)
    y_own = call(
        margin_kernel,
        (
            point_ids, paths, vol_surface, chol_factor, generator.reshape(1, NF), exposure_load,
            reset_load, bstart,
        ),
        [((2, STEPS), F32)],
        "margins",
        cost=(STEPS * NF * (NF + 256) * 2, 4 * MIB),
        vmem=60,
        grid=(chunks,),
        in_specs=[
            pl.BlockSpec(memory_space=pltpu.SMEM), row_spec, row_spec, square, full((1, NF)),
            full((NB, NF)), full((NB, NF)), full((1, NB)),
        ],
        out_specs=pl.BlockSpec((2, CHUNK), lambda i: (0, i)),
    )
    y0 = lax.all_gather(y_own, TM, axis=0)
    moved = lax.optimization_barrier((y0, *moved))[1:]
    pair = jnp.where(lax.axis_index("x1") == 0, jnp.stack(moved), jnp.stack(moved[::-1]))
    basis = lax.all_gather(pair, "z", axis=0, tiled=True).reshape(2, 2, 2, 2, 64, STEPS)

    s2 = [swap(vol_a, "yl"), swap(after(vol_b, y0), "yl")]
    s1 = [swap(v, "c") for v in lax.optimization_barrier((vol_a, vol_b, y0))[:2]]
    s3 = [swap(v, "c") for v in s2]

    kept, o1, o2, o3, wt, bmat = call(
        sens_kernel,
        (y0, paths, vol_surface, chol_factor, exposure_load) + rows,
        [((256, NF), F32)] + [((256, NF), BF)] * 3 + [((WROWS, STEPS), BF), ((WROWS, NF), BF)],
        "sensitivities",
        cost=(STEPS * NF * (NF + 256) * 2, 5 * MIB),
        grid=(chunks,),
    )
    g1, g2, g3 = (shift_x(o, d + 1) for d, o in enumerate((o1, o2, o3)))

    ck, cs = call(
        chol_kernel,
        (after(wt, pair), bmat, paths, vol_surface),
        [((256, NF), F32)] * 2,
        "chol_term",
        cost=(STEPS * NF * (NF + 256) * 2, 5 * MIB),
        grid=(chunks,),
        in_specs=[full((WROWS, STEPS)), full((WROWS, NF)), row_spec, row_spec],
        scratch=[pltpu.VMEM((NF, NF), F32)],
    )
    ck, cs = call(
        chol_split_kernel, (ck, swap(cs, "c")), [((128, NF), F32)] * 2, "chol_split", cost=(0, MIB)
    )
    cg = swap(cs, "yl")

    peers = [(a * 2 + b, (1 - a) * 2 + 1 - b) for a in range(2) for b in range(2)]
    y = exchange(jnp.broadcast_to(y0[None], (GROUP,) + y0.shape), PEERS)
    cols, radj = call(
        points_kernel,
        (y,) + rows,
        [((BLOCKS, STEPS, 2 * GROUP), F32), ((GROUP, NB, NF), F32)],
        "points",
        cost=(0, 6 * MIB),
    )

    kept = after(kept, y)
    parts = call(
        sum_x_kernel, (kept, g1, g2, g3, ck, cg), [((8, 48, NF), BF)], "sum_x", cost=(0, 2 * MIB)
    )
    parts = after(exchange(parts, "z"), cols)
    part = call(sum_z_kernel, (parts,), [((48, NF), F32)], "sum_z", cost=(0, MIB // 2))
    got = swap(part, "yh")
    total = call(total_kernel, (part, got), [((8, 48, NF), BF)], "totals", cost=(0, MIB // 2))
    mine = call(
        gather_z_kernel, (exchange(total, "z"),), [((384, NF), BF)], "gather_z", cost=(0, MIB)
    )
    own, o1, o2, o3 = call(
        adjoint_kernel,
        (basis, vol_surface, *s1, *s2, *s3, cols, radj, chol_factor, exposure_load, bstart),
        [((ROWS, NF), F32)] + [((ROWS, NF), BF)] * 3,
        "adjoints",
        cost=(7 * STEPS * STEPS * NF * 2, 12 * MIB),
        vmem=56,
        in_specs=[pl.BlockSpec(memory_space=pl.ANY)] * 8
        + [full(cols.shape), full(radj.shape), square, full((NB, NF)), full((1, NB))],
        scratch=[
            pltpu.VMEM((2, STEPS, GROUP * NF), BF),
            pltpu.VMEM((ROWS, GROUP * NF), F32),
            pltpu.VMEM((BLOCKS, 2, 2, 64, STEPS), BF),
            pltpu.VMEM((STEPS, NF), F32),
            pltpu.VMEM((BLOCKS - 1, STEPS, NF), BF),
            pltpu.SemaphoreType.DMA((11,)),
        ],
    )
    vol_greeks, quarter = call(
        greeks_kernel,
        [after(mine, own)] + [shift_x(mine, d) for d in range(1, 4)],
        [((STEPS, NF), F32), ((128, NF), BF)],
        "greeks",
        cost=(0, 4 * MIB),
    )
    halved = call(
        chol_half_kernel, (quarter, swap(quarter, "yl")), [((256, NF), BF)], "chol_half", cost=(0, MIB)
    )
    chol_greeks = call(
        chol_out_kernel, (halved, swap(halved, "c")), [((NF, NF), F32)], "chol_out", cost=(0, 2 * MIB)
    )

    normals = call(
        normals_kernel,
        (own, swap(o1, "x0"), swap(o2, "yh"), lax.ppermute(o3, PEERS, peers)),
        [((STEPS * 4, 128), F32)],
        "normals",
        cost=(0, 4 * MIB),
    )
    return normals.reshape(STEPS, 1, NF), vol_greeks, chol_greeks


def solution(mesh):
    split = Mesh(mesh.devices.reshape(2, 2, 2, 8, 2, 2), ALL)
    return jax.shard_map(
        body,
        mesh=split,
        in_specs=(
            P(TM, PTS, None),
            P(PTS, TM),
            P(TM, None),
            P(),
            P(),
            P(),
            P(),
            P(),
            P(),
            P(),
            P(PTS),
        ),
        out_specs=(P(TM, PTS, None), P(TM, None), P()),
        check_vma=False,
    )
```

profile of v0, /device:TPU:2, one launch (start us, length us, event | category | flops | bytes accessed | tf_op | source)
XLA Modules:
  0.0 161.2 jit_solution(4751318185521504450)
XLA Ops:
  7.2 0.0 all-gather.4.cloned.1.call-start
  7.2 2.9 %collective-permute-start.1 = (bf16[64,1024]{1,0:T(8,128)(2,1)}, bf16[64,1024]{1,0:T(8,128)(2,1)S(1)}, u32[]{:S(2)}, u32[]{:S(2)}) collective-permute-start(bf16[64,1024]{1,0:T(8,128)(2,1)} %param.12), channel_id=1, source_target_pairs={{0,2},{1,6},{2,0},{3,4},{4,3},{5,7},{6,1},{7,5},{8,34},{9,38},{10,... | collective-permute-start | bytes 393224 | tf_op jit(solution)/shard_map/ppermute | solution.py:389
  10.1 3.2 %collective-permute-start = (bf16[64,1024]{1,0:T(8,128)(2,1)}, bf16[64,1024]{1,0:T(8,128)(2,1)}, u32[]{:S(2)}, u32[]{:S(2)}) collective-permute-start(bf16[64,1024]{1,0:T(8,128)(2,1)} %param.12), channel_id=1, source_target_pairs={{0,0},{1,4},{2,2},{3,6},{4,1},{5,5},{6,3},{7,7},{8,32},{9,36},{10,... | collective-permute-start | bytes 393224 | tf_op jit(solution)/shard_map/ppermute | solution.py:389
  14.0 0.0 copy-start
  14.1 0.0 copy-start.5
  14.1 0.0 copy-start.6
  14.1 5.8 %margins.1 = f32[2,1024]{1,0:T(2,128)} custom-call(s32[1]{0:T(128)S(6)} %copy.16.pid, bf16[1024,512]{1,0:T(8,128)(2,1)} %bitcast.10, f32[1024,512]{1,0:T(8,128)} %vol.5, bf16[512,512]{1,0:T(8,128)(2,1)} %chol.5, s32[1,512]{1,0:T(1,128)} %bitcast.24, f32[32,512]{1,0:T(8,128)} %load.5, f32[32,512]{1,0:T(8,128)} %reset.5, s32[1,32]{1,0:T(1,128)} %bitcast.13), custom_call_target="tpu_custom_call" | custom-call | flops 805306368 | bytes 4194304 | tf_op jit(solution)/shard_map/margins/pallas_call | solution.py:330
  19.9 12.7 %all-gather.1.y = f32[4,2,1024]{2,1,0:T(2,128)S(1)} all-gather(f32[1,2,1024]{2,1,0:T(2,128)} %bitcast.23), channel_id=2, replica_groups=mesh['yl'=2,'c'=2,'yh'=2,'z'=8,'x1'=2,'x0'=2] {'yl','c'}, dimensions={0}, use_global_device_ids=true | all-gather | bytes 40960 | tf_op jit(solution)/shard_map/all_gather | solution.py:412
  32.6 0.0 collective-permute-done.1
  32.6 0.0 collective-permute-done
  32.6 1.7 %maximum_select_fusion = bf16[2,64,1024]{2,1,0:T(8,128)(2,1)} fusion(bf16[1,64,1024]{2,1,0:T(8,128)(2,1)S(1)} %bitcast.22, bf16[1,64,1024]{2,1,0:T(8,128)(2,1)} %bitcast.4, pred[]{:T(512)S(6)} %eq.3), kind=kLoop, calls=%fused_computation | loop fusion | flops 393216 | bytes 524289 | tf_op jit(solution)/shard_map/jit(_where)/select_n | solution.py:414
  34.4 0.0 all-gather.4.cloned.1.call-update
  34.5 0.0 copy-start.2
  34.5 1.0 copy-done.2
  35.5 2.4 %sensitivities.1 = (f32[256,512]{1,0:T(8,128)S(1)}, bf16[256,512]{1,0:T(8,128)(2,1)S(1)}, bf16[256,512]{1,0:T(8,128)(2,1)S(1)}, bf16[256,512]{1,0:T(8,128)(2,1)S...) custom-call(f32[4,2,1024]{2,1,0:T(2,128)S(1)} %all-gather.1.y, bf16[1024,512]{1,0:T(8,128)(2,1)S(1)} %bitcast.11, ...), custom_call_target="tpu_custom_call" | custom-call | flops 805306368 | bytes 5242880 | tf_op jit(solution)/shard_map/sensitivities/pallas_call | solution.py:330
  37.9 2.7 %chol_term.1 = (f32[256,512]{1,0:T(8,128)S(1)}, f32[256,512]{1,0:T(8,128)S(1)}) custom-call(bf16[160,1024]{1,0:T(8,128)(2,1)S(1)} %get-tuple-element.47.wt, bf16[160,512]{1,0:T(8,128)(2,1)S(1)} %get-tuple-element.48.bmat, bf16[1024,512]{1,0:T(8,128)(2,1)S(1)} %bitcast.12, f32[1024,512]{1,0:T(8,128)S(1)} %copy-done), custom_call_target="tpu_custom_call" | custom-call | flops 805306368 | bytes 5242880 | tf_op jit(solution)/shard_map/chol_term/pallas_call | solution.py:330
  40.7 0.4 collective-permute-start.14
  41.1 2.9 %collective-permute-start.12 = (bf16[256,512]{1,0:T(8,128)(2,1)S(1)}, bf16[256,512]{1,0:T(8,128)(2,1)S(1)}, u32[]{:S(2)}, u32[]{:S(2)}) collective-permute-start(bf16[256,512]{1,0:T(8,128)(2,1)S(1)} %get-tuple-element.44), channel_id=1, source_target_pairs={{0,2},{1,3},{2,0},{3,1},{4,6},{5,7},{6,4},{7,5},{8,10},{9,11},{10,... | collective-permute-start | bytes 786440 | tf_op jit(solution)/shard_map/ppermute | solution.py:361
  44.0 0.0 collective-permute-start.13
  44.0 0.0 collective-permute-done.14.got
  44.0 0.1 chol_split.1
  44.0 0.7 collective-permute-start.15
  44.8 12.1 %all_to_all.15.y = f32[4,4,2,1024]{3,2,1,0:T(2,128)S(1)} all-to-all(f32[4,4,2,1024]{3,2,1,0:T(2,128)S(1)} %broadcast_in_dim.2), channel_id=1, replica_groups=mesh['yl'=2,'c'=2,'yh'=2,'z'=8,'x1'=2,'x0'=2] {'yh','x0'}, dimensions={0} | all-to-all | bytes 262144 | tf_op jit(solution)/shard_map/all_to_all | solution.py:365
  56.9 0.0 collective-permute-done.11.g1
  56.9 0.0 collective-permute-done.12.g2
  56.9 0.9 sum_x.1
  57.8 6.0 %all-to-all-start.1 = ((bf16[8,48,512]{2,1,0:T(8,128)(2,1)}), bf16[8,48,512]{2,1,0:T(8,128)(2,1)S(1)}, u32[]{:S(2)}, u32[]{:S(2)}) async-start(bf16[8,48,512]{2,1,0:T(8,128)(2,1)} %sum_x.1), calls=%async_computation.1 | async-start | bytes 786432 | tf_op jit(solution)/shard_map/all_to_all | solution.py:365
  63.8 0.1 convert.4
  64.0 0.9 fusion
  64.8 0.1 collective-permute-start.5
  65.0 1.9 %collective-permute-start.4 = (bf16[512,512]{1,0:T(8,128)(2,1)}, bf16[512,512]{1,0:T(8,128)(2,1)}, u32[]{:S(2)}, u32[]{:S(2)}) collective-permute-start(bf16[512,512]{1,0:T(8,128)(2,1)} %get-tuple-element.32), channel_id=1, source_target_pairs={{0,128},{128,0},{1,129},{129,1},{2,130},{130,2},{3,131},{131,3},{4... | collective-permute-start | bytes 1572872 | tf_op jit(solution)/shard_map/ppermute | solution.py:357
  66.8 1.5 points.1
  68.4 0.0 copy-start.9
  68.4 1.3 copy-done.9
  69.7 9.1 %all-to-all-done.1.parts = bf16[8,48,512]{2,1,0:T(8,128)(2,1)S(1)} async-done(((bf16[8,48,512]{2,1,0:T(8,128)(2,1)}), bf16[8,48,512]{2,1,0:T(8,128)(2,1)S(1)}, u32[]{:S(2)}, u32[]{:S(2)}) %all-to-all-start.1) | async-done | bytes 393248 | tf_op jit(solution)/shard_map/all_to_all | solution.py:365
  78.8 0.1 sum_z.1.own
  78.9 3.4 %collective-permute-start.16 = (f32[48,512]{1,0:T(8,128)S(1)}, f32[48,512]{1,0:T(8,128)S(1)}, u32[]{:S(2)}, u32[]{:S(2)}) collective-permute-start(f32[48,512]{1,0:T(8,128)S(1)} %sum_z.1.own), channel_id=1, source_target_pairs={{0,32},{32,0},{1,33},{33,1},{2,34},{34,2},{3,35},{35,3},{4,36},{36... | collective-permute-start | bytes 294920 | tf_op jit(solution)/shard_map/ppermute | solution.py:357
  82.3 9.2 %collective-permute-done.16.got = f32[48,512]{1,0:T(8,128)S(1)} collective-permute-done((f32[48,512]{1,0:T(8,128)S(1)}, f32[48,512]{1,0:T(8,128)S(1)}, u32[]{:S(2)}, u32[]{:S(2)}) %collective-permute-start.16) | collective-permute-done | bytes 98336 | tf_op jit(solution)/shard_map/ppermute | solution.py:357
  91.5 0.8 totals.1
  92.3 6.9 %all-to-all-start.2 = ((bf16[8,48,512]{2,1,0:T(8,128)(2,1)}), bf16[8,48,512]{2,1,0:T(8,128)(2,1)S(1)}, u32[]{:S(2)}, u32[]{:S(2)}) async-start(bf16[8,48,512]{2,1,0:T(8,128)(2,1)} %totals.1), calls=%async_computation.2 | async-start | bytes 786432 | tf_op jit(solution)/shard_map/all_to_all | solution.py:365
  99.2 0.0 collective-permute-start.2
  99.2 0.5 collective-permute-start.3
  99.7 0.1 collective-permute-start.7
  99.8 0.4 collective-permute-start.6
  100.2 11.1 %all-to-all-done.2.parts = bf16[8,48,512]{2,1,0:T(8,128)(2,1)S(1)} async-done(((bf16[8,48,512]{2,1,0:T(8,128)(2,1)}), bf16[8,48,512]{2,1,0:T(8,128)(2,1)S(1)}, u32[]{:S(2)}, u32[]{:S(2)}) %all-to-all-start.2) | async-done | bytes 393248 | tf_op jit(solution)/shard_map/all_to_all | solution.py:365
  111.4 2.0 %collective-permute-start.19 = (bf16[384,512]{1,0:T(8,128)(2,1)S(1)}, bf16[384,512]{1,0:T(8,128)(2,1)S(1)}, u32[]{:S(2)}, u32[]{:S(2)}) collective-permute-start(bf16[384,512]{1,0:T(8,128)(2,1)S(1)} %gather_z.1.own), channel_id=1, source_target_pairs={{0,3},{1,0},{2,1},{3,2},{4,7},{5,4},{6,5},{7,6},{8,11},{9,8},{10,9... | collective-permute-start | bytes 1179656 | tf_op jit(solution)/shard_map/ppermute | solution.py:361
  113.4 0.0 collective-permute-done.2.s1a
  113.4 1.7 %collective-permute-start.18 = (bf16[384,512]{1,0:T(8,128)(2,1)S(1)}, bf16[384,512]{1,0:T(8,128)(2,1)S(1)}, u32[]{:S(2)}, u32[]{:S(2)}) collective-permute-start(bf16[384,512]{1,0:T(8,128)(2,1)S(1)} %gather_z.1.own), channel_id=1, source_target_pairs={{0,2},{1,3},{2,0},{3,1},{4,6},{5,7},{6,4},{7,5},{8,10},{9,11},{10,... | collective-permute-start | bytes 1179656 | tf_op jit(solution)/shard_map/ppermute | solution.py:361
  115.0 2.5 %collective-permute-start.17 = (bf16[384,512]{1,0:T(8,128)(2,1)S(1)}, bf16[384,512]{1,0:T(8,128)(2,1)S(1)}, u32[]{:S(2)}, u32[]{:S(2)}) collective-permute-start(bf16[384,512]{1,0:T(8,128)(2,1)S(1)} %gather_z.1.own), channel_id=1, source_target_pairs={{0,1},{1,2},{2,3},{3,0},{4,5},{5,6},{6,7},{7,4},{8,9},{9,10},{10,1... | collective-permute-start | bytes 1179656 | tf_op jit(solution)/shard_map/ppermute | solution.py:361
  117.6 15.5 %adjoints.1 = (f32[256,512]{1,0:T(8,128)}, bf16[256,512]{1,0:T(8,128)(2,1)}, bf16[256,512]{1,0:T(8,128)(2,1)}, bf16[256,512]{1,0:T(8,128)(2,1)}) custom-call(bf16[2,2,2,2,64,1024]{5,4,3,2,1,0:T(8,128)(2,1)} %bitcast.25, f32[1024,512]{1,0:T(8,128)} %vol.5, bf16[512,512]{1,0:T(8,128)(2,1)} %copy-done.11, bf16[512,512]{1,0:T(8,128)(2,1)} %copy-done.12, ...), custom_call_target="tpu_custom_call" | custom-call | flops 7516192768 | bytes 12582912 | tf_op jit(solution)/shard_map/adjoints/pallas_call | solution.py:330
  133.1 0.0 collective-permute-done.19.g3
  133.2 1.5 greeks.1
  134.6 0.6 collective-permute-start.20
  135.2 0.2 collective-permute-start.8
  135.4 2.4 %collective-permute-start.9 = (bf16[256,512]{1,0:T(8,128)(2,1)}, bf16[256,512]{1,0:T(8,128)(2,1)S(1)}, u32[]{:S(2)}, u32[]{:S(2)}) collective-permute-start(bf16[256,512]{1,0:T(8,128)(2,1)} %get-tuple-element.39), channel_id=1, source_target_pairs={{0,32},{32,0},{1,33},{33,1},{2,34},{34,2},{3,35},{35,3},{4,36},{36... | collective-permute-start | bytes 786440 | tf_op jit(solution)/shard_map/ppermute | solution.py:357
  137.9 2.4 %collective-permute-start.10 = (bf16[256,512]{1,0:T(8,128)(2,1)}, bf16[256,512]{1,0:T(8,128)(2,1)S(1)}, u32[]{:S(2)}, u32[]{:S(2)}) collective-permute-start(bf16[256,512]{1,0:T(8,128)(2,1)} %get-tuple-element.40), channel_id=1, source_target_pairs={{0,33},{1,32},{32,1},{33,0},{2,35},{3,34},{34,3},{35,2},{4,37},{5,... | collective-permute-start | bytes 786440 | tf_op jit(solution)/shard_map/ppermute | solution.py:501
  140.2 0.7 collective-permute-done.20.got
  141.0 0.1 collective-permute-start.21
  141.1 2.3 %collective-permute-done.8.g1 = bf16[256,512]{1,0:T(8,128)(2,1)S(1)} collective-permute-done((bf16[256,512]{1,0:T(8,128)(2,1)}, bf16[256,512]{1,0:T(8,128)(2,1)S(1)}, u32[]{:S(2)}, u32[]{:S(2)}) %collective-permute-start.8) | collective-permute-done | bytes 262176 | tf_op jit(solution)/shard_map/ppermute | solution.py:357
  143.4 8.2 %collective-permute-done.9.g2 = bf16[256,512]{1,0:T(8,128)(2,1)S(1)} collective-permute-done((bf16[256,512]{1,0:T(8,128)(2,1)}, bf16[256,512]{1,0:T(8,128)(2,1)S(1)}, u32[]{:S(2)}, u32[]{:S(2)}) %collective-permute-start.9) | collective-permute-done | bytes 262176 | tf_op jit(solution)/shard_map/ppermute | solution.py:357
  151.7 0.0 collective-permute-done.10.g3
  151.7 1.6 normals.1
  153.3 0.0 collective-permute-done.21.got
  153.3 1.0 chol_out.1
  (33 shorter events, 0.2 us)
Async XLA Ops:
  7.2 110.4 %all-gather.4.cloned.1.call-start = ((), (), s32[]{:S(2)}) async-start(), calls=%async_computation.3 | async-start | bytes 2359296 | tf_op jit(solution)/shard_map/all_gather | solution.py:415
  7.2 25.4 %collective-permute-start.1 = (bf16[64,1024]{1,0:T(8,128)(2,1)}, bf16[64,1024]{1,0:T(8,128)(2,1)S(1)}, u32[]{:S(2)}, u32[]{:S(2)}) collective-permute-start(bf16[64,1024]{1,0:T(8,128)(2,1)} %param.12), channel_id=1, source_target_pairs={{0,2},{1,6},{2,0},{3,4},{4,3},{5,7},{6,1},{7,5},{8,34},{9,38},{10,... | collective-permute-start | bytes 393224 | tf_op jit(solution)/shard_map/ppermute | solution.py:389
  10.1 22.5 %collective-permute-start = (bf16[64,1024]{1,0:T(8,128)(2,1)}, bf16[64,1024]{1,0:T(8,128)(2,1)}, u32[]{:S(2)}, u32[]{:S(2)}) collective-permute-start(bf16[64,1024]{1,0:T(8,128)(2,1)} %param.12), channel_id=1, source_target_pairs={{0,0},{1,4},{2,2},{3,6},{4,1},{5,5},{6,3},{7,7},{8,32},{9,36},{10,... | collective-permute-start | bytes 393224 | tf_op jit(solution)/shard_map/ppermute | solution.py:389
  14.0 20.4 %copy-start = (f32[1024,512]{1,0:T(8,128)S(1)}, f32[1024,512]{1,0:T(8,128)}, u32[]{:S(2)}) copy-start(f32[1024,512]{1,0:T(8,128)} %vol.5) | copy-start | bytes 6291460
  14.1 20.3 %copy-start.1 = (bf16[1024,1,512]{2,0,1:T(8,128)(2,1)S(1)}, bf16[1024,1,512]{2,0,1:T(8,128)(2,1)}, u32[]{:S(2)}) copy-start(bf16[1024,1,512]{2,0,1:T(8,128)(2,1)} %param.11) | copy-start | bytes 3145732
  14.1 20.3 %copy-start.3 = (f32[32,512]{1,0:T(8,128)S(1)}, f32[32,512]{1,0:T(8,128)}, u32[]{:S(2)}) copy-start(f32[32,512]{1,0:T(8,128)} %reset.5) | copy-start | bytes 196612
  14.1 20.3 %copy-start.5 = (f32[32,512]{1,0:T(8,128)S(1)}, f32[32,512]{1,0:T(8,128)}, u32[]{:S(2)}) copy-start(f32[32,512]{1,0:T(8,128)} %load.5) | copy-start | bytes 196612
  14.1 20.3 %copy-start.6 = (s32[32]{0:T(128)S(1)}, s32[32]{0:T(128)}, u32[]{:S(2)}) copy-start(s32[32]{0:T(128)} %param.19) | copy-start | bytes 388
  14.1 20.3 %copy-start.7 = (f32[32]{0:T(128)S(1)}, f32[32]{0:T(128)}, u32[]{:S(2)}) copy-start(f32[32]{0:T(128)} %param.17) | copy-start | bytes 388
  14.1 20.3 %copy-start.8 = (f32[32]{0:T(128)S(1)}, f32[32]{0:T(128)}, u32[]{:S(2)}) copy-start(f32[32]{0:T(128)} %param.18) | copy-start | bytes 388
  34.5 1.0 copy-start.2
  40.7 3.3 %collective-permute-start.14 = (f32[256,512]{1,0:T(8,128)S(1)}, f32[256,512]{1,0:T(8,128)S(1)}, u32[]{:S(2)}, u32[]{:S(2)}) collective-permute-start(f32[256,512]{1,0:T(8,128)S(1)} %get-tuple-element.50), channel_id=1, source_target_pairs={{0,64},{64,0},{1,65},{65,1},{2,66},{66,2},{3,67},{67,3},{4,68},{68... | collective-permute-start | bytes 1572872 | tf_op jit(solution)/shard_map/ppermute | solution.py:357
  41.1 15.8 %collective-permute-start.11 = (bf16[256,512]{1,0:T(8,128)(2,1)S(1)}, bf16[256,512]{1,0:T(8,128)(2,1)S(1)}, u32[]{:S(2)}, u32[]{:S(2)}) collective-permute-start(bf16[256,512]{1,0:T(8,128)(2,1)S(1)} %get-tuple-element.43), channel_id=1, source_target_pairs={{0,1},{1,2},{2,3},{3,0},{4,5},{5,6},{6,7},{7,4},{8,9},{9,10},{10,1... | collective-permute-start | bytes 786440 | tf_op jit(solution)/shard_map/ppermute | solution.py:361
  41.1 15.8 %collective-permute-start.12 = (bf16[256,512]{1,0:T(8,128)(2,1)S(1)}, bf16[256,512]{1,0:T(8,128)(2,1)S(1)}, u32[]{:S(2)}, u32[]{:S(2)}) collective-permute-start(bf16[256,512]{1,0:T(8,128)(2,1)S(1)} %get-tuple-element.44), channel_id=1, source_target_pairs={{0,2},{1,3},{2,0},{3,1},{4,6},{5,7},{6,4},{7,5},{8,10},{9,11},{10,... | collective-permute-start | bytes 786440 | tf_op jit(solution)/shard_map/ppermute | solution.py:361
  44.0 12.9 %collective-permute-start.13 = (bf16[256,512]{1,0:T(8,128)(2,1)S(1)}, bf16[256,512]{1,0:T(8,128)(2,1)S(1)}, u32[]{:S(2)}, u32[]{:S(2)}) collective-permute-start(bf16[256,512]{1,0:T(8,128)(2,1)S(1)} %get-tuple-element.45), channel_id=1, source_target_pairs={{0,3},{1,0},{2,1},{3,2},{4,7},{5,4},{6,5},{7,6},{8,11},{9,8},{10,9... | collective-permute-start | bytes 786440 | tf_op jit(solution)/shard_map/ppermute | solution.py:361
  44.0 12.9 %collective-permute-start.15 = (f32[128,512]{1,0:T(8,128)S(1)}, f32[128,512]{1,0:T(8,128)S(1)}, u32[]{:S(2)}, u32[]{:S(2)}) collective-permute-start(f32[128,512]{1,0:T(8,128)S(1)} %get-tuple-element.52), channel_id=1, source_target_pairs={{0,128},{128,0},{1,129},{129,1},{2,130},{130,2},{3,131},{131,3},{4... | collective-permute-start | bytes 786440 | tf_op jit(solution)/shard_map/ppermute | solution.py:357
  57.8 21.0 %all-to-all-start.1 = ((bf16[8,48,512]{2,1,0:T(8,128)(2,1)}), bf16[8,48,512]{2,1,0:T(8,128)(2,1)S(1)}, u32[]{:S(2)}, u32[]{:S(2)}) async-start(bf16[8,48,512]{2,1,0:T(8,128)(2,1)} %sum_x.1), calls=%async_computation.1 | async-start | bytes 786432 | tf_op jit(solution)/shard_map/all_to_all | solution.py:365
  64.8 34.9 %collective-permute-start.5 = (bf16[512,512]{1,0:T(8,128)(2,1)S(1)}, bf16[512,512]{1,0:T(8,128)(2,1)}, u32[]{:S(2)}, u32[]{:S(2)}) collective-permute-start(bf16[512,512]{1,0:T(8,128)(2,1)S(1)} %get-tuple-element.34), channel_id=1, source_target_pairs={{0,128},{128,0},{1,129},{129,1},{2,130},{130,2},{3,131},{131,3},{4... | collective-permute-start | bytes 1572872 | tf_op jit(solution)/shard_map/ppermute | solution.py:357
  65.0 34.8 %collective-permute-start.4 = (bf16[512,512]{1,0:T(8,128)(2,1)}, bf16[512,512]{1,0:T(8,128)(2,1)}, u32[]{:S(2)}, u32[]{:S(2)}) collective-permute-start(bf16[512,512]{1,0:T(8,128)(2,1)} %get-tuple-element.32), channel_id=1, source_target_pairs={{0,128},{128,0},{1,129},{129,1},{2,130},{130,2},{3,131},{131,3},{4... | collective-permute-start | bytes 1572872 | tf_op jit(solution)/shard_map/ppermute | solution.py:357
  68.4 1.3 copy-start.9
  69.7 47.9 %copy-start.10 = (f32[4,32,512]{2,1,0:T(8,128)}, f32[4,32,512]{2,1,0:T(8,128)S(1)}, u32[]{:S(2)}) copy-start(f32[4,32,512]{2,1,0:T(8,128)S(1)} %get-tuple-element.36.radj) | copy-start | bytes 786436
  78.9 12.6 %collective-permute-start.16 = (f32[48,512]{1,0:T(8,128)S(1)}, f32[48,512]{1,0:T(8,128)S(1)}, u32[]{:S(2)}, u32[]{:S(2)}) collective-permute-start(f32[48,512]{1,0:T(8,128)S(1)} %sum_z.1.own), channel_id=1, source_target_pairs={{0,32},{32,0},{1,33},{33,1},{2,34},{34,2},{3,35},{35,3},{4,36},{36... | collective-permute-start | bytes 294920 | tf_op jit(solution)/shard_map/ppermute | solution.py:357
  92.3 19.1 %all-to-all-start.2 = ((bf16[8,48,512]{2,1,0:T(8,128)(2,1)}), bf16[8,48,512]{2,1,0:T(8,128)(2,1)S(1)}, u32[]{:S(2)}, u32[]{:S(2)}) async-start(bf16[8,48,512]{2,1,0:T(8,128)(2,1)} %totals.1), calls=%async_computation.2 | async-start | bytes 786432 | tf_op jit(solution)/shard_map/all_to_all | solution.py:365
  99.2 14.2 %collective-permute-start.2 = (bf16[512,512]{1,0:T(8,128)(2,1)}, bf16[512,512]{1,0:T(8,128)(2,1)S(1)}, u32[]{:S(2)}, u32[]{:S(2)}) collective-permute-start(bf16[512,512]{1,0:T(8,128)(2,1)} %get-tuple-element.32), channel_id=1, source_target_pairs={{0,64},{64,0},{1,65},{65,1},{2,66},{66,2},{3,67},{67,3},{4,68},{68... | collective-permute-start | bytes 1572872 | tf_op jit(solution)/shard_map/ppermute | solution.py:357
  99.2 15.8 %collective-permute-start.3 = (bf16[512,512]{1,0:T(8,128)(2,1)S(1)}, bf16[512,512]{1,0:T(8,128)(2,1)S(1)}, u32[]{:S(2)}, u32[]{:S(2)}) collective-permute-start(bf16[512,512]{1,0:T(8,128)(2,1)S(1)} %get-tuple-element.34), channel_id=1, source_target_pairs={{0,64},{64,0},{1,65},{65,1},{2,66},{66,2},{3,67},{67,3},{4,68},{68... | collective-permute-start | bytes 1572872 | tf_op jit(solution)/shard_map/ppermute | solution.py:357
  99.7 17.8 %collective-permute-start.7 = (bf16[512,512]{1,0:T(8,128)(2,1)}, bf16[512,512]{1,0:T(8,128)(2,1)}, u32[]{:S(2)}, u32[]{:S(2)}) collective-permute-start(bf16[512,512]{1,0:T(8,128)(2,1)} %collective-permute-done.5.s2b), channel_id=1, source_target_pairs={{0,64},{64,0},{1,65},{65,1},{2,66},{66,2},{3,67},{67,3},{4,68},{68... | collective-permute-start | bytes 1572872 | tf_op jit(solution)/shard_map/ppermute | solution.py:357
  99.8 17.8 %collective-permute-start.6 = (bf16[512,512]{1,0:T(8,128)(2,1)}, bf16[512,512]{1,0:T(8,128)(2,1)}, u32[]{:S(2)}, u32[]{:S(2)}) collective-permute-start(bf16[512,512]{1,0:T(8,128)(2,1)} %collective-permute-done.4.s2a), channel_id=1, source_target_pairs={{0,64},{64,0},{1,65},{65,1},{2,66},{66,2},{3,67},{67,3},{4,68},{68... | collective-permute-start | bytes 1572872 | tf_op jit(solution)/shard_map/ppermute | solution.py:357
  111.4 21.8 %collective-permute-start.19 = (bf16[384,512]{1,0:T(8,128)(2,1)S(1)}, bf16[384,512]{1,0:T(8,128)(2,1)S(1)}, u32[]{:S(2)}, u32[]{:S(2)}) collective-permute-start(bf16[384,512]{1,0:T(8,128)(2,1)S(1)} %gather_z.1.own), channel_id=1, source_target_pairs={{0,3},{1,0},{2,1},{3,2},{4,7},{5,4},{6,5},{7,6},{8,11},{9,8},{10,9... | collective-permute-start | bytes 1179656 | tf_op jit(solution)/shard_map/ppermute | solution.py:361
  113.4 4.2 %copy-start.11 = (bf16[512,512]{1,0:T(8,128)(2,1)}, bf16[512,512]{1,0:T(8,128)(2,1)S(1)}, u32[]{:S(2)}) copy-start(bf16[512,512]{1,0:T(8,128)(2,1)S(1)} %collective-permute-done.2.s1a) | copy-start | bytes 1572868
  113.4 19.8 %collective-permute-start.18 = (bf16[384,512]{1,0:T(8,128)(2,1)S(1)}, bf16[384,512]{1,0:T(8,128)(2,1)S(1)}, u32[]{:S(2)}, u32[]{:S(2)}) collective-permute-start(bf16[384,512]{1,0:T(8,128)(2,1)S(1)} %gather_z.1.own), channel_id=1, source_target_pairs={{0,2},{1,3},{2,0},{3,1},{4,6},{5,7},{6,4},{7,5},{8,10},{9,11},{10,... | collective-permute-start | bytes 1179656 | tf_op jit(solution)/shard_map/ppermute | solution.py:361
  115.0 2.6 %copy-start.12 = (bf16[512,512]{1,0:T(8,128)(2,1)}, bf16[512,512]{1,0:T(8,128)(2,1)S(1)}, u32[]{:S(2)}) copy-start(bf16[512,512]{1,0:T(8,128)(2,1)S(1)} %collective-permute-done.3.s1b) | copy-start | bytes 1572868
  115.0 18.1 %collective-permute-start.17 = (bf16[384,512]{1,0:T(8,128)(2,1)S(1)}, bf16[384,512]{1,0:T(8,128)(2,1)S(1)}, u32[]{:S(2)}, u32[]{:S(2)}) collective-permute-start(bf16[384,512]{1,0:T(8,128)(2,1)S(1)} %gather_z.1.own), channel_id=1, source_target_pairs={{0,1},{1,2},{2,3},{3,0},{4,5},{5,6},{6,7},{7,4},{8,9},{9,10},{10,1... | collective-permute-start | bytes 1179656 | tf_op jit(solution)/shard_map/ppermute | solution.py:361
  133.1 18.5 %copy-start.4 = (f32[256,512]{1,0:T(8,128)S(1)}, f32[256,512]{1,0:T(8,128)}, u32[]{:S(2)}) copy-start(f32[256,512]{1,0:T(8,128)} %get-tuple-element.37.own) | copy-start | bytes 1572868
  134.6 6.3 %collective-permute-start.20 = (bf16[128,512]{1,0:T(8,128)(2,1)S(1)}, bf16[128,512]{1,0:T(8,128)(2,1)S(1)}, u32[]{:S(2)}, u32[]{:S(2)}) collective-permute-start(bf16[128,512]{1,0:T(8,128)(2,1)S(1)} %get-tuple-element.56.own), channel_id=1, source_target_pairs={{0,128},{128,0},{1,129},{129,1},{2,130},{130,2},{3,131},{131,3},{4... | collective-permute-start | bytes 393224 | tf_op jit(solution)/shard_map/ppermute | solution.py:357
  135.2 8.2 %collective-permute-start.8 = (bf16[256,512]{1,0:T(8,128)(2,1)}, bf16[256,512]{1,0:T(8,128)(2,1)S(1)}, u32[]{:S(2)}, u32[]{:S(2)}) collective-permute-start(bf16[256,512]{1,0:T(8,128)(2,1)} %get-tuple-element.38), channel_id=1, source_target_pairs={{0,1},{1,0},{2,3},{3,2},{4,5},{5,4},{6,7},{7,6},{8,9},{9,8},{10,11... | collective-permute-start | bytes 786440 | tf_op jit(solution)/shard_map/ppermute | solution.py:357
  135.4 16.2 %collective-permute-start.9 = (bf16[256,512]{1,0:T(8,128)(2,1)}, bf16[256,512]{1,0:T(8,128)(2,1)S(1)}, u32[]{:S(2)}, u32[]{:S(2)}) collective-permute-start(bf16[256,512]{1,0:T(8,128)(2,1)} %get-tuple-element.39), channel_id=1, source_target_pairs={{0,32},{32,0},{1,33},{33,1},{2,34},{34,2},{3,35},{35,3},{4,36},{36... | collective-permute-start | bytes 786440 | tf_op jit(solution)/shard_map/ppermute | solution.py:357
  137.9 13.8 %collective-permute-start.10 = (bf16[256,512]{1,0:T(8,128)(2,1)}, bf16[256,512]{1,0:T(8,128)(2,1)S(1)}, u32[]{:S(2)}, u32[]{:S(2)}) collective-permute-start(bf16[256,512]{1,0:T(8,128)(2,1)} %get-tuple-element.40), channel_id=1, source_target_pairs={{0,33},{1,32},{32,1},{33,0},{2,35},{3,34},{34,3},{35,2},{4,37},{5,... | collective-permute-start | bytes 786440 | tf_op jit(solution)/shard_map/ppermute | solution.py:501
  141.0 12.3 %collective-permute-start.21 = (bf16[256,512]{1,0:T(8,128)(2,1)S(1)}, bf16[256,512]{1,0:T(8,128)(2,1)S(1)}, u32[]{:S(2)}, u32[]{:S(2)}) collective-permute-start(bf16[256,512]{1,0:T(8,128)(2,1)S(1)} %chol_half.1.own), channel_id=1, source_target_pairs={{0,64},{64,0},{1,65},{65,1},{2,66},{66,2},{3,67},{67,3},{4,68},{68... | collective-permute-start | bytes 786440 | tf_op jit(solution)/shard_map/ppermute | solution.py:357
Sparse Core Ops, SparseCore 0:
  34.5 43.3 all-gather.3
where the time goes:
time: 162 us; the launch traced here: 161 us
  starting transfers between devices  41.4 us (26%)
  waiting for transfers between devices  40.8 us (25%)
  Pallas kernels  33.9 us (21%)
  blocking collectives  24.9 us (15%)
  between operations  15 us (9%)
  local copies, waits for them, and re-layouts  3.3 us (2%)
  other arithmetic  1.86 us (1%)
    pallas_call x14, Pallas kernels, call(): pl.pallas_call(kernel, out_shape=shapes[0] if single else shapes, scratch...  33.9 us
    ppermute x13, waiting for transfers between devices, swap(): return lax.ppermute(x, axis, [(0, 1), (1, 0)])  20.6 us
    all_to_all x2, waiting for transfers between devices, exchange(): return lax.all_to_all(x, axes, split_axis=0, concat_axis=0, tiled=True)  20.2 us
    all_to_all x2, starting transfers between devices, exchange(): return lax.all_to_all(x, axes, split_axis=0, concat_axis=0, tiled=True)  13 us
    all_gather x1, blocking collectives, body(): y0 = lax.all_gather(y_own, TM, axis=0)  12.7 us
    all_to_all x1, blocking collectives, exchange(): return lax.all_to_all(x, axes, split_axis=0, concat_axis=0, tiled=True)  12.1 us
    ppermute x13, starting transfers between devices, swap(): return lax.ppermute(x, axis, [(0, 1), (1, 0)])  10.8 us
    ppermute x6, starting transfers between devices, shift_x(): return lax.ppermute(x, X, [(i, (i + d) % 4) for i in range(4)])  9.08 us
  transfers between devices with their start and end apart: 25, of which 6 were waited for; matrix products, arithmetic and copies ran while one was open for 1% of the time, Pallas kernels for 19%

commit v1 on v0

--- a/solution.py
+++ b/solution.py
@@ -8,11 +8,12 @@
 BF = jnp.bfloat16
 F32 = jnp.float32
 I32 = jnp.int32
-ALL = ("yl", "c", "yh", "z", "x1", "x0")
+ALL = ("yl", "c", "yh", "z2", "z1", "z0", "x1", "x0")
 TM = ("yl", "c")
 X = ("x1", "x0")
-PTS = ("yh", "z", "x1", "x0")
-PEERS = ("yh", "x0")
+Z = ("z2", "z1", "z0")
+PTS = ("yh",) + Z + X
+PEERS = ("yh", "z0")
 NB = 32
 STEPS = 1024
 BLOCKS = 4
@@ -74,8 +75,9 @@
     return lax.axis_index("yl") * 2 + lax.axis_index("c")
 
 
-def margin_kernel(pid, paths, vol, chol, gen, load, reset, bstart, out):
+def margin_kernel(pid, paths, vol, chol, gen, load, reset, bstart, out, vol_bf):
     i = pl.program_id(0)
+    vol_bf[...] = vol[...].astype(BF)
     low = (pid[0] * (gen[...] & 1023)) & 1048575
     high = ((pid[0] * (gen[...] >> 10)) & 1023) << 10
     residue = (low + high) & 1048575
@@ -100,7 +102,7 @@
 
 
 def group_index():
-    return lax.axis_index("yh") * 2 + lax.axis_index("x0")
+    return lax.axis_index("yh") * 2 + lax.axis_index("z0")
 
 
 def bucket_values(y, hots, strikes, weight):
@@ -257,48 +259,54 @@
 
 
 def adjoint_kernel(
-    basis_hbm, vol_hbm, s1a, s1b, s2a, s2b, s3a, s3b, cols, radj, chol, load, bstart,
-    own, o1, o2, o3, scaled, acc, basis, vol, vols, sems,
+    b0, b1, b2, b3, vol_hbm, s1, s2a, s2b, s3a, s3b, cols, radj, chol, load, bstart,
+    own, o1, o2, o3, scaled, acc, basis, vol, vols, vol_load, sems,
 ):
     half = STEPS // 2
     copies = [[pltpu.make_async_copy(vol_hbm, vol, sems.at[0])]]
-    for r, pair in enumerate(((s1a, s1b), (s2a, s2b), (s3a, s3b))):
+    copies.append([pltpu.make_async_copy(s1, vols.at[0], sems.at[1])])
+    for r, pair in enumerate(((s2a, s2b), (s3a, s3b))):
         copies.append(
             [
-                pltpu.make_async_copy(p, vols.at[r, pl.ds(h * half, half)], sems.at[1 + 2 * r + h])
+                pltpu.make_async_copy(p, vols.at[r + 1, pl.ds(h * half, half)], sems.at[2 + 2 * r + h])
                 for h, p in enumerate(pair)
             ]
         )
+    z2, z1, x = lax.axis_index("z2"), lax.axis_index("z1"), x_index()
     for r in range(BLOCKS):
-        source = basis_hbm.at[r & 1, r >> 1]
-        copies[r].append(pltpu.make_async_copy(source, basis.at[r], sems.at[7 + r]))
+        piece = ((r & 1) ^ z1) * 2 + ((r >> 1) ^ z2)
+        for d, b in enumerate((b0, b1, b2, b3)):
+            place = basis.at[r, lax.rem(x + 4 - d, 4)]
+            copies[r].append(pltpu.make_async_copy(b.at[piece], place, sems.at[6 + 4 * r + d]))
         for copy in copies[r]:
             copy.start()
     start, nxt = bucket_ends(bstart[...])
     load_parts = jnp.concatenate(split3(load[...]), axis=0)
     at_resets = jnp.zeros((ROWS, NB), F32)
     vol_resets = jnp.zeros((NB, NF), F32)
-    for r in range(BLOCKS):
-        for copy in copies[r]:
-            copy.wait()
-        b = own_block() ^ r
-        member, at_start = one_hots(b * STEPS, STEPS, start, nxt)
-        member, at_start = member.astype(BF), at_start.astype(BF)
-        for j in range(STEPS // CHUNK):
-            rows = slice(j * CHUNK, (j + 1) * CHUNK)
-            v = vols[r - 1, rows, :] if r else vol[rows, :]
-            hot = member[:, rows]
-            loads = dot(jnp.concatenate([hot, hot, hot], axis=0), load_parts, TN)
-            vol_load = v.astype(F32) * loads
-            for q in range(GROUP):
-                part = vol_load * cols[b, rows, q : q + 1]
-                scaled[r % 2, rows, q * NF : (q + 1) * NF] = part.astype(BF)
-            for h in (v,) if r else split2(v):
-                vol_resets = vol_resets + dot(at_start[:, rows], h, NN)
-        lhs = jnp.concatenate([basis[r, x & 1, x >> 1] for x in range(4)], axis=0)
-        new = dot(lhs, scaled[r % 2], NN)
-        acc[...] = new if r == 0 else acc[...] + new
-        at_resets = at_resets + dot(lhs, at_start, NT)
+    for r in range(BLOCKS + 1):
+        if r < BLOCKS:
+            for copy in copies[r]:
+                copy.wait()
+            b = own_block() ^ r
+            member, at_start = one_hots(b * STEPS, STEPS, start, nxt)
+            member, at_start = member.astype(BF), at_start.astype(BF)
+            hots = jnp.concatenate([member] * 3, axis=0)
+            at_resets = at_resets + dot(basis[r].reshape(ROWS, STEPS), at_start, NT)
+        for q in range(GROUP):
+            cut = slice(q * NF, (q + 1) * NF)
+            for j in range(STEPS // CHUNK if r < BLOCKS else 0):
+                rows = slice(j * CHUNK, (j + 1) * CHUNK)
+                if q == 0:
+                    v = vols[r - 1, rows, :] if r else vol[rows, :]
+                    for h in (v,) if r else split2(v):
+                        vol_resets = vol_resets + dot(at_start[:, rows], h, NN)
+                    vol_load[rows, :] = v.astype(F32) * dot(hots[:, rows], load_parts, TN)
+                part = vol_load[rows, :] * cols[b, rows, q : q + 1]
+                scaled[r % 2, rows, cut] = part.astype(BF)
+            if r:
+                new = dot(basis[r - 1].reshape(ROWS, STEPS), scaled[1 - r % 2, :, cut], NN)
+                acc[:, cut] = new if r == 1 else acc[:, cut] + new
     at_resets = at_resets.astype(BF)
     for q, o in enumerate((own, o1, o2, o3)):
         more = dot(at_resets, (vol_resets * radj[q]).astype(BF), NN)
@@ -347,9 +355,8 @@
                     for x in range(4):
                         src = (((yl * 2 + c) * 2 + yh) * 8 + z) * 4 + x
                         z2, z1, z0 = z >> 2, (z >> 1) & 1, z & 1
-                        to_z = (c ^ z2) * 4 + (yl ^ yh) * 2 + (x & 1)
-                        to_x = ((x >> 1) ^ d) * 2 + z0
-                        moves.append((src, (((yh * 2 + z2) * 2 + z1) * 8 + to_z) * 4 + to_x))
+                        to_z = (yl ^ yh ^ d) * 4 + (c ^ z2) * 2 + z0
+                        moves.append((src, (((yh * 2 + z2) * 2 + z1) * 8 + to_z) * 4 + x))
     return moves
 
 
@@ -390,15 +397,13 @@
     chunks = STEPS // CHUNK
     row_spec = pl.BlockSpec((CHUNK, NF), lambda i: (i, 0))
     square = full((NF, NF))
-    vol_a = vol_surface[: STEPS // 2].astype(BF)
-    vol_b = vol_surface[STEPS // 2 :].astype(BF)
-    y_own = call(
+    y_own, vol_bf = call(
         margin_kernel,
         (
             point_ids, paths, vol_surface, chol_factor, generator.reshape(1, NF), exposure_load,
             reset_load, bstart,
         ),
-        [((2, STEPS), F32)],
+        [((2, STEPS), F32), ((STEPS, NF), BF)],
         "margins",
         cost=(STEPS * NF * (NF + 256) * 2, 4 * MIB),
         vmem=60,
@@ -407,16 +412,11 @@
             pl.BlockSpec(memory_space=pltpu.SMEM), row_spec, row_spec, square, full((1, NF)),
             full((NB, NF)), full((NB, NF)), full((1, NB)),
         ],
-        out_specs=pl.BlockSpec((2, CHUNK), lambda i: (0, i)),
+        out_specs=[pl.BlockSpec((2, CHUNK), lambda i: (0, i)), row_spec],
     )
     y0 = lax.all_gather(y_own, TM, axis=0)
-    moved = lax.optimization_barrier((y0, *moved))[1:]
-    pair = jnp.where(lax.axis_index("x1") == 0, jnp.stack(moved), jnp.stack(moved[::-1]))
-    basis = lax.all_gather(pair, "z", axis=0, tiled=True).reshape(2, 2, 2, 2, 64, STEPS)
-
-    s2 = [swap(vol_a, "yl"), swap(after(vol_b, y0), "yl")]
-    s1 = [swap(v, "c") for v in lax.optimization_barrier((vol_a, vol_b, y0))[:2]]
-    s3 = [swap(v, "c") for v in s2]
+    y0, *moved = lax.optimization_barrier((y0, *moved))
+    moved = jnp.stack(moved)
 
     kept, o1, o2, o3, wt, bmat = call(
         sens_kernel,
@@ -430,7 +430,7 @@
 
     ck, cs = call(
         chol_kernel,
-        (after(wt, pair), bmat, paths, vol_surface),
+        (wt, bmat, paths, vol_surface),
         [((256, NF), F32)] * 2,
         "chol_term",
         cost=(STEPS * NF * (NF + 256) * 2, 5 * MIB),
@@ -443,6 +443,10 @@
     )
     cg = swap(cs, "yl")
 
+    vol_a, vol_b = vol_bf[: STEPS // 2], vol_bf[STEPS // 2 :]
+    s2 = [swap(after(vol_a, y0), "yl"), swap(after(vol_b, cg), "yl")]
+    s1 = swap(after(vol_bf, cg), "c")
+    s3 = [swap(v, "c") for v in s2]
     peers = [(a * 2 + b, (1 - a) * 2 + 1 - b) for a in range(2) for b in range(2)]
     y = exchange(jnp.broadcast_to(y0[None], (GROUP,) + y0.shape), PEERS)
     cols, radj = call(
@@ -453,38 +457,45 @@
         cost=(0, 6 * MIB),
     )
 
-    kept = after(kept, y)
+    quad = jnp.concatenate([moved, swap(moved, "z1")])
+
+    kept = after(kept, s2[0], y)
     parts = call(
         sum_x_kernel, (kept, g1, g2, g3, ck, cg), [((8, 48, NF), BF)], "sum_x", cost=(0, 2 * MIB)
     )
-    parts = after(exchange(parts, "z"), cols)
+    basis = [quad] + [shift_x(after(quad, parts), d) for d in range(1, 4)]
+    parts = after(exchange(parts, Z), cols, s2[1])
     part = call(sum_z_kernel, (parts,), [((48, NF), F32)], "sum_z", cost=(0, MIB // 2))
-    got = swap(part, "yh")
+    got = after(swap(part, "yh"), basis[1], basis[3])
     total = call(total_kernel, (part, got), [((8, 48, NF), BF)], "totals", cost=(0, MIB // 2))
-    mine = call(
-        gather_z_kernel, (exchange(total, "z"),), [((384, NF), BF)], "gather_z", cost=(0, MIB)
-    )
     own, o1, o2, o3 = call(
         adjoint_kernel,
-        (basis, vol_surface, *s1, *s2, *s3, cols, radj, chol_factor, exposure_load, bstart),
+        (*basis, vol_surface, s1, *s2, *s3, cols, radj, chol_factor, exposure_load, bstart),
         [((ROWS, NF), F32)] + [((ROWS, NF), BF)] * 3,
         "adjoints",
         cost=(7 * STEPS * STEPS * NF * 2, 12 * MIB),
         vmem=56,
-        in_specs=[pl.BlockSpec(memory_space=pl.ANY)] * 8
+        in_specs=[pl.BlockSpec(memory_space=pl.ANY)] * 10
         + [full(cols.shape), full(radj.shape), square, full((NB, NF)), full((1, NB))],
         scratch=[
             pltpu.VMEM((2, STEPS, GROUP * NF), BF),
             pltpu.VMEM((ROWS, GROUP * NF), F32),
-            pltpu.VMEM((BLOCKS, 2, 2, 64, STEPS), BF),
+            pltpu.VMEM((BLOCKS, 4, 64, STEPS), BF),
             pltpu.VMEM((STEPS, NF), F32),
             pltpu.VMEM((BLOCKS - 1, STEPS, NF), BF),
-            pltpu.SemaphoreType.DMA((11,)),
+            pltpu.VMEM((STEPS, NF), F32),
+            pltpu.SemaphoreType.DMA((22,)),
         ],
     )
+    mine = call(
+        gather_z_kernel, (after(exchange(total, Z), basis[2]),), [((384, NF), BF)], "gather_z", cost=(0, MIB)
+    )
+    spread = [mine] + [shift_x(mine, d) for d in range(1, 4)]
+    others = swap(o1, "z0"), swap(o2, "yh"), lax.ppermute(o3, PEERS, peers)
+    spread[0] = after(mine, own)
     vol_greeks, quarter = call(
         greeks_kernel,
-        [after(mine, own)] + [shift_x(mine, d) for d in range(1, 4)],
+        spread,
         [((STEPS, NF), F32), ((128, NF), BF)],
         "greeks",
         cost=(0, 4 * MIB),
@@ -498,7 +509,7 @@
 
     normals = call(
         normals_kernel,
-        (own, swap(o1, "x0"), swap(o2, "yh"), lax.ppermute(o3, PEERS, peers)),
+        (own, *others),
         [((STEPS * 4, 128), F32)],
         "normals",
         cost=(0, 4 * MIB),
@@ -507,7 +518,7 @@
 
 
 def solution(mesh):
-    split = Mesh(mesh.devices.reshape(2, 2, 2, 8, 2, 2), ALL)
+    split = Mesh(mesh.devices.reshape((2,) * 8), ALL)
     return jax.shard_map(
         body,
         mesh=split,

time: 162 us -> 143 us (0.88)
  blocking collectives: 24.9 us -> 7.11 us
  between operations: 15 us -> 1.61 us
  starting transfers between devices: 41.4 us -> 54.4 us
  waiting for transfers between devices: 40.8 us -> 38.7 us
    all_to_all x2 -> x3, waiting for transfers between devices: 20.2 us -> 6.8 us  [exchange(): return lax.all_to_all(x, axes, split_axis=0, concat_axis=0, tiled=True)]
    all_to_all x1 -> x0, blocking collectives: 12.1 us -> none  [exchange(): return lax.all_to_all(x, axes, split_axis=0, concat_axis=0, tiled=True)]
    ppermute x6 -> x9, waiting for transfers between devices: 0.02 us -> 10.3 us  [shift_x(): return lax.ppermute(x, X, [(i, (i + d) % 4) for i in range(4)])]
    all_gather x1, blocking collectives: 12.7 us -> 7.11 us  [body(): y0 = lax.all_gather(y_own, TM, axis=0)]
    ppermute x2, starting transfers between devices: 6.17 us -> 11.5 us  [body(): moved = [lax.ppermute(pca_basis, ALL, basis_moves(d)) for d in range(2)]]
    ppermute x13, starting transfers between devices: 10.8 us -> 15.1 us  [swap(): return lax.ppermute(x, axis, [(0, 1), (1, 0)])]
    ppermute x6 -> x9, starting transfers between devices: 9.08 us -> 13.2 us  [shift_x(): return lax.ppermute(x, X, [(i, (i + d) % 4) for i in range(4)])]
    ppermute x1, starting transfers between devices: 2.36 us -> 0.01 us  [body(): others = (swap(o1, 'z0'), swap(o2, 'yh'), lax.ppermute(o3, PEERS, peers))]
  transfers between devices with their start and end apart: 25 -> 28, of which waited for: 6 -> 12; matrix products, arithmetic and copies ran while one was open for 1% -> 3% of each run, Pallas kernels for 19% -> 18%
where the time goes in v1:
time: 143 us; the launch traced here: 142 us
  starting transfers between devices  54.4 us (38%)
  waiting for transfers between devices  38.7 us (27%)
  Pallas kernels  33.7 us (24%)
  blocking collectives  7.11 us (5%)
  local copies, waits for them, and re-layouts  3.72 us (3%)
  other arithmetic  2.8 us (2%)
  between operations  1.61 us (1%)
    pallas_call x14, Pallas kernels, call(): pl.pallas_call(kernel, out_shape=shapes[0] if single else shapes, scratch...  33.7 us
    ppermute x13, waiting for transfers between devices, swap(): return lax.ppermute(x, axis, [(0, 1), (1, 0)])  19.6 us
    ppermute x13, starting transfers between devices, swap(): return lax.ppermute(x, axis, [(0, 1), (1, 0)])  15.1 us
    all_to_all x3, starting transfers between devices, exchange(): return lax.all_to_all(x, axes, split_axis=0, concat_axis=0, tiled=True)  14.5 us
    ppermute x9, starting transfers between devices, shift_x(): return lax.ppermute(x, X, [(i, (i + d) % 4) for i in range(4)])  13.2 us
    ppermute x2, starting transfers between devices, body(): moved = [lax.ppermute(pca_basis, ALL, basis_moves(d)) for d in range(2)]  11.5 us
    ppermute x9, waiting for transfers between devices, shift_x(): return lax.ppermute(x, X, [(i, (i + d) % 4) for i in range(4)])  10.3 us
    all_gather x1, blocking collectives, body(): y0 = lax.all_gather(y_own, TM, axis=0)  7.11 us
  transfers between devices with their start and end apart: 28, of which 12 were waited for; matrix products, arithmetic and copies ran while one was open for 3% of the time, Pallas kernels for 18%

profile of v1, /device:TPU:2, one launch (start us, length us, event | category | flops | bytes accessed | tf_op | source)
XLA Modules:
  0.0 142.0 jit_solution(13675754203954644138)
XLA Ops:
  0.6 0.0 copy-start
  0.7 0.0 copy-start.7
  0.7 0.0 copy-start.2
  0.7 0.0 copy-start.8
  0.7 9.4 %collective-permute-start.1 = (bf16[64,1024]{1,0:T(8,128)(2,1)}, bf16[64,1024]{1,0:T(8,128)(2,1)}, u32[]{:S(2)}, u32[]{:S(2)}) collective-permute-start(bf16[64,1024]{1,0:T(8,128)(2,1)} %param.12), channel_id=1, source_target_pairs={{0,16},{1,17},{2,18},{3,19},{4,20},{5,21},{6,22},{7,23},{8,48},{9,... | collective-permute-start | bytes 393224 | tf_op jit(solution)/shard_map/ppermute | solution.py:396
  10.1 2.2 %collective-permute-start = (bf16[64,1024]{1,0:T(8,128)(2,1)}, bf16[64,1024]{1,0:T(8,128)(2,1)}, u32[]{:S(2)}, u32[]{:S(2)}) collective-permute-start(bf16[64,1024]{1,0:T(8,128)(2,1)} %param.12), channel_id=1, source_target_pairs={{0,0},{1,1},{2,2},{3,3},{4,4},{5,5},{6,6},{7,7},{8,32},{9,33},{10,... | collective-permute-start | bytes 393224 | tf_op jit(solution)/shard_map/ppermute | solution.py:396
  12.9 5.8 %margins.1 = (f32[2,1024]{1,0:T(2,128)}, bf16[1024,512]{1,0:T(8,128)(2,1)}) custom-call(s32[1]{0:T(128)S(6)} %copy.16.pid, bf16[1024,512]{1,0:T(8,128)(2,1)} %bitcast.9, f32[1024,512]{1,0:T(8,128)} %vol_hbm.1, bf16[512,512]{1,0:T(8,128)(2,1)} %chol.5, s32[1,512]{1,0:T(1,128)} %bitcast.22, f32[32,512]{1,0:T(8,128)} %load.5, f32[32,512]{1,0:T(8,128)} %reset.5, ...), custom_call_target="tpu_custom_call" | custom-call | flops 805306368 | bytes 4194304 | tf_op jit(solution)/shard_map/margins/pallas_call | solution.py:338
  18.7 7.1 %all-gather.1.y = f32[4,2,1024]{2,1,0:T(2,128)S(1)} all-gather(f32[1,2,1024]{2,1,0:T(2,128)} %bitcast.21), channel_id=2, replica_groups=mesh['yl'=2,'c'=2,'yh'=2,'z2'=2,'z1'=2,'z0'=2,'x1'=2,'x0'=2] {'yl','c'}, dimensions={0}, use_global_device_ids=true | all-gather | bytes 40960 | tf_op jit(solution)/shard_map/all_gather | solution.py:417
  25.9 3.2 %sensitivities.1 = (f32[256,512]{1,0:T(8,128)S(1)}, bf16[256,512]{1,0:T(8,128)(2,1)}, bf16[256,512]{1,0:T(8,128)(2,1)}, bf16[256,512]{1,0:T(8,128)(2,1)S(1)}, bf...) custom-call(f32[4,2,1024]{2,1,0:T(2,128)S(1)} %all-gather.1.y, bf16[1024,512]{1,0:T(8,128)(2,1)S(1)} %bitcast.10, ...), custom_call_target="tpu_custom_call" | custom-call | flops 805306368 | bytes 5242880 | tf_op jit(solution)/shard_map/sensitivities/pallas_call | solution.py:338
  29.2 0.8 copy-done.4
  29.9 2.7 %chol_term.1 = (f32[256,512]{1,0:T(8,128)S(1)}, f32[256,512]{1,0:T(8,128)S(1)}) custom-call(bf16[160,1024]{1,0:T(8,128)(2,1)S(1)} %get-tuple-element.46.wt, bf16[160,512]{1,0:T(8,128)(2,1)S(1)} %get-tuple-element.47.bmat, bf16[1024,512]{1,0:T(8,128)(2,1)S(1)} %bitcast.11, f32[1024,512]{1,0:T(8,128)S(1)} %copy-done), custom_call_target="tpu_custom_call" | custom-call | flops 805306368 | bytes 5242880 | tf_op jit(solution)/shard_map/chol_term/pallas_call | solution.py:338
  32.7 0.0 copy-start.5
  32.7 0.3 collective-permute-start.7
  33.0 0.8 fusion
  33.8 1.5 %collective-permute-start.3 = (bf16[512,512]{1,0:T(8,128)(2,1)S(1)}, bf16[512,512]{1,0:T(8,128)(2,1)}, u32[]{:S(2)}, u32[]{:S(2)}) collective-permute-start(bf16[512,512]{1,0:T(8,128)(2,1)S(1)} %get-tuple-element.41), channel_id=1, source_target_pairs={{0,128},{128,0},{1,129},{129,1},{2,130},{130,2},{3,131},{131,3},{4... | collective-permute-start | bytes 1572872 | tf_op jit(solution)/shard_map/ppermute | solution.py:364
  35.3 1.5 %collective-permute-start.4 = (bf16[256,512]{1,0:T(8,128)(2,1)}, bf16[256,512]{1,0:T(8,128)(2,1)S(1)}, u32[]{:S(2)}, u32[]{:S(2)}) collective-permute-start(bf16[256,512]{1,0:T(8,128)(2,1)} %get-tuple-element.43), channel_id=1, source_target_pairs={{0,1},{1,2},{2,3},{3,0},{4,5},{5,6},{6,7},{7,4},{8,9},{9,10},{10,1... | collective-permute-start | bytes 786440 | tf_op jit(solution)/shard_map/ppermute | solution.py:368
  36.7 1.1 collective-permute-start.5
  37.9 2.2 %collective-permute-start.6 = (bf16[256,512]{1,0:T(8,128)(2,1)S(1)}, bf16[256,512]{1,0:T(8,128)(2,1)S(1)}, u32[]{:S(2)}, u32[]{:S(2)}) collective-permute-start(bf16[256,512]{1,0:T(8,128)(2,1)S(1)} %get-tuple-element.45), channel_id=1, source_target_pairs={{0,3},{1,0},{2,1},{3,2},{4,7},{5,4},{6,5},{7,6},{8,11},{9,8},{10,9... | collective-permute-start | bytes 786440 | tf_op jit(solution)/shard_map/ppermute | solution.py:368
  40.0 0.1 chol_split.1
  40.1 0.7 collective-permute-start.8
  40.8 0.7 broadcast_in_dim.2
  41.4 3.3 %all-to-all-start = ((f32[4,4,2,1024]{3,2,1,0:T(2,128)}), f32[4,4,2,1024]{3,2,1,0:T(2,128)S(1)}, u32[]{:S(2)}, u32[]{:S(2)}) async-start(f32[4,4,2,1024]{3,2,1,0:T(2,128)} %broadcast_in_dim.2), calls=%async_computation | async-start | bytes 262144 | tf_op jit(solution)/shard_map/all_to_all | solution.py:372
  44.8 1.7 %pad_maximum_fusion.1 = bf16[2,64,1024]{2,1,0:T(8,128)(2,1)} fusion(bf16[1,64,1024]{2,1,0:T(8,128)(2,1)} %bitcast.5, bf16[1,64,1024]{2,1,0:T(8,128)(2,1)} %bitcast.4), kind=kLoop, calls=%fused_computation.1 | loop fusion | flops 131072 | bytes 524288 | tf_op jit(solution)/shard_map/stack | solution.py:419
  46.5 2.6 %collective-permute-done.3.s2a = bf16[512,512]{1,0:T(8,128)(2,1)} collective-permute-done((bf16[512,512]{1,0:T(8,128)(2,1)S(1)}, bf16[512,512]{1,0:T(8,128)(2,1)}, u32[]{:S(2)}, u32[]{:S(2)}) %collective-permute-start.3) | collective-permute-done | bytes 524320 | tf_op jit(solution)/shard_map/ppermute | solution.py:364
  49.0 1.4 %collective-permute-start.2 = (bf16[2,64,1024]{2,1,0:T(8,128)(2,1)}, bf16[2,64,1024]{2,1,0:T(8,128)(2,1)}, u32[]{:S(2)}, u32[]{:S(2)}) collective-permute-start(bf16[2,64,1024]{2,1,0:T(8,128)(2,1)} %pad_maximum_fusion.1), channel_id=1, source_target_pairs={{0,8},{8,0},{1,9},{9,1},{2,10},{10,2},{3,11},{11,3},{4,12},{12,4},... | collective-permute-start | bytes 786440 | tf_op jit(solution)/shard_map/ppermute | solution.py:364
  50.4 5.7 %all-to-all-done.y = f32[4,4,2,1024]{3,2,1,0:T(2,128)S(1)} async-done(((f32[4,4,2,1024]{3,2,1,0:T(2,128)}), f32[4,4,2,1024]{3,2,1,0:T(2,128)S(1)}, u32[]{:S(2)}, u32[]{:S(2)}) %all-to-all-start) | async-done | bytes 131104 | tf_op jit(solution)/shard_map/all_to_all | solution.py:372
  56.2 0.0 copy-start.14
  56.2 0.9 sum_x.1
  57.1 5.4 %all-to-all-start.1 = ((bf16[8,48,512]{2,1,0:T(8,128)(2,1)}), bf16[8,48,512]{2,1,0:T(8,128)(2,1)S(1)}, u32[]{:S(2)}, u32[]{:S(2)}) async-start(bf16[8,48,512]{2,1,0:T(8,128)(2,1)} %sum_x.1), calls=%async_computation.1 | async-start | bytes 786432 | tf_op jit(solution)/shard_map/all_to_all | solution.py:372
  62.4 0.1 collective-permute-start.13
  62.5 0.5 collective-permute-done.2
  63.0 1.1 pad_maximum_fusion.b0
  64.1 0.0 copy-start.15
  64.1 0.3 collective-permute-start.11
  64.4 1.8 %collective-permute-start.9 = (bf16[4,64,1024]{2,1,0:T(8,128)(2,1)S(1)}, bf16[4,64,1024]{2,1,0:T(8,128)(2,1)}, u32[]{:S(2)}, u32[]{:S(2)}) collective-permute-start(bf16[4,64,1024]{2,1,0:T(8,128)(2,1)S(1)} %pad_maximum_fusion.b0), channel_id=1, source_target_pairs={{0,1},{1,2},{2,3},{3,0},{4,5},{5,6},{6,7},{7,4},{8,9},{9,10},{10,1... | collective-permute-start | bytes 1572872 | tf_op jit(solution)/shard_map/ppermute | solution.py:368
  66.2 1.5 %points.1 = (f32[4,1024,8]{2,1,0:T(8,128)S(1)}, f32[4,32,512]{2,1,0:T(8,128)S(1)}) custom-call(f32[4,4,2,1024]{3,2,1,0:T(2,128)S(1)} %all-to-all-done.y, f32[32,512]{1,0:T(8,128)S(1)} %copy-done.3, f32[1,32]{1,0:T(1,128)S(1)} %bitcast.17, f32[1,32]{1,0:T(1,128)S(1)} %bitcast.19, s32[1,32]{1,0:T(1,128)S(1)} %bitcast.15), custom_call_target="tpu_custom_call" | custom-call | bytes 6291456 | tf_op jit(solution)/shard_map/points/pallas_call | solution.py:338
  67.7 0.0 copy-start.11
  67.8 1.3 copy-done.11
  69.1 6.2 %collective-permute-done.13.s2b = bf16[512,512]{1,0:T(8,128)(2,1)S(1)} collective-permute-done((bf16[512,512]{1,0:T(8,128)(2,1)}, bf16[512,512]{1,0:T(8,128)(2,1)S(1)}, u32[]{:S(2)}, u32[]{:S(2)}) %collective-permute-start.13) | collective-permute-done | bytes 524320 | tf_op jit(solution)/shard_map/ppermute | solution.py:364
  75.3 1.1 all-to-all-done.1.parts
  76.3 0.1 sum_z.1.own
  76.4 2.5 %collective-permute-start.19 = (f32[48,512]{1,0:T(8,128)S(1)}, f32[48,512]{1,0:T(8,128)S(1)}, u32[]{:S(2)}, u32[]{:S(2)}) collective-permute-start(f32[48,512]{1,0:T(8,128)S(1)} %sum_z.1.own), channel_id=1, source_target_pairs={{0,32},{32,0},{1,33},{33,1},{2,34},{34,2},{3,35},{35,3},{4,36},{36... | collective-permute-start | bytes 294920 | tf_op jit(solution)/shard_map/ppermute | solution.py:364
  78.9 0.4 collective-permute-done.9.b1
  79.3 3.5 %collective-permute-done.19.got = f32[48,512]{1,0:T(8,128)S(1)} collective-permute-done((f32[48,512]{1,0:T(8,128)S(1)}, f32[48,512]{1,0:T(8,128)S(1)}, u32[]{:S(2)}, u32[]{:S(2)}) %collective-permute-start.19) | collective-permute-done | bytes 98336 | tf_op jit(solution)/shard_map/ppermute | solution.py:364
  82.8 0.8 totals.1
  83.6 5.8 %all-to-all-start.2 = ((bf16[8,48,512]{2,1,0:T(8,128)(2,1)}), bf16[8,48,512]{2,1,0:T(8,128)(2,1)S(1)}, u32[]{:S(2)}, u32[]{:S(2)}) async-start(bf16[8,48,512]{2,1,0:T(8,128)(2,1)} %totals.1), calls=%async_computation.2 | async-start | bytes 786432 | tf_op jit(solution)/shard_map/all_to_all | solution.py:372
  89.4 2.1 %collective-permute-start.10 = (bf16[4,64,1024]{2,1,0:T(8,128)(2,1)S(1)}, bf16[4,64,1024]{2,1,0:T(8,128)(2,1)}, u32[]{:S(2)}, u32[]{:S(2)}) collective-permute-start(bf16[4,64,1024]{2,1,0:T(8,128)(2,1)S(1)} %pad_maximum_fusion.b0), channel_id=1, source_target_pairs={{0,2},{1,3},{2,0},{3,1},{4,6},{5,7},{6,4},{7,5},{8,10},{9,11},{10,... | collective-permute-start | bytes 1572872 | tf_op jit(solution)/shard_map/ppermute | solution.py:368
  91.5 0.5 collective-permute-start.15
  92.0 9.9 %collective-permute-done.10.b2 = bf16[4,64,1024]{2,1,0:T(8,128)(2,1)} collective-permute-done((bf16[4,64,1024]{2,1,0:T(8,128)(2,1)S(1)}, bf16[4,64,1024]{2,1,0:T(8,128)(2,1)}, u32[]{:S(2)}, u32[]{:S(2)}) %collective-permute-start.10) | collective-permute-done | bytes 524320 | tf_op jit(solution)/shard_map/ppermute | solution.py:368
  102.0 1.1 collective-permute-start.22
  103.1 1.2 collective-permute-start.21
  104.4 1.9 %collective-permute-start.20 = (bf16[384,512]{1,0:T(8,128)(2,1)S(1)}, bf16[384,512]{1,0:T(8,128)(2,1)S(1)}, u32[]{:S(2)}, u32[]{:S(2)}) collective-permute-start(bf16[384,512]{1,0:T(8,128)(2,1)S(1)} %gather_z.1.own), channel_id=1, source_target_pairs={{0,1},{1,2},{2,3},{3,0},{4,5},{5,6},{6,7},{7,4},{8,9},{9,10},{10,1... | collective-permute-start | bytes 1179656 | tf_op jit(solution)/shard_map/ppermute | solution.py:368
  106.2 14.5 %adjoints.1 = (f32[256,512]{1,0:T(8,128)}, bf16[256,512]{1,0:T(8,128)(2,1)}, bf16[256,512]{1,0:T(8,128)(2,1)}, bf16[256,512]{1,0:T(8,128)(2,1)}) custom-call(bf16[4,64,1024]{2,1,0:T(8,128)(2,1)} %copy-done.15, bf16[4,64,1024]{2,1,0:T(8,128)(2,1)} %collective-permute-done.9.b1, bf16[4,64,1024]{2,1,0:T(8,128)(2,1)} %collective-permute-done.10.b2, ...), custom_call_target="tpu_custom_call" | custom-call | flops 7516192768 | bytes 12582912 | tf_op jit(solution)/shard_map/adjoints/pallas_call | solution.py:338
  120.8 1.5 %greeks.1 = (f32[1024,512]{1,0:T(8,128)}, bf16[128,512]{1,0:T(8,128)(2,1)S(1)}) custom-call(bf16[384,512]{1,0:T(8,128)(2,1)S(1)} %gather_z.1.own, bf16[384,512]{1,0:T(8,128)(2,1)S(1)} %collective-permute-done.20.g1, bf16[384,512]{1,0:T(8,128)(2,1)S(1)} %collective-permute-done.21.g2, bf16[384,512]{1,0:T(8,128)(2,1)S(1)} %collective-permute-done.22.g3), custom_call_target="tpu_custom_call" | custom-call | bytes 4194304 | tf_op jit(solution)/shard_map/greeks/pallas_call | solution.py:338
  122.3 2.0 %collective-permute-start.23 = (bf16[128,512]{1,0:T(8,128)(2,1)S(1)}, bf16[128,512]{1,0:T(8,128)(2,1)S(1)}, u32[]{:S(2)}, u32[]{:S(2)}) collective-permute-start(bf16[128,512]{1,0:T(8,128)(2,1)S(1)} %get-tuple-element.66.own), channel_id=1, source_target_pairs={{0,128},{128,0},{1,129},{129,1},{2,130},{130,2},{3,131},{131,3},{4... | collective-permute-start | bytes 393224 | tf_op jit(solution)/shard_map/ppermute | solution.py:364
  124.2 2.0 %collective-permute-start.16 = (bf16[256,512]{1,0:T(8,128)(2,1)}, bf16[256,512]{1,0:T(8,128)(2,1)S(1)}, u32[]{:S(2)}, u32[]{:S(2)}) collective-permute-start(bf16[256,512]{1,0:T(8,128)(2,1)} %get-tuple-element.58), channel_id=1, source_target_pairs={{0,4},{4,0},{1,5},{5,1},{2,6},{6,2},{3,7},{7,3},{8,12},{12,8},{9,1... | collective-permute-start | bytes 786440 | tf_op jit(solution)/shard_map/ppermute | solution.py:364
  126.3 4.1 %collective-permute-start.17 = (bf16[256,512]{1,0:T(8,128)(2,1)}, bf16[256,512]{1,0:T(8,128)(2,1)S(1)}, u32[]{:S(2)}, u32[]{:S(2)}) collective-permute-start(bf16[256,512]{1,0:T(8,128)(2,1)} %get-tuple-element.59), channel_id=1, source_target_pairs={{0,32},{32,0},{1,33},{33,1},{2,34},{34,2},{3,35},{35,3},{4,36},{36... | collective-permute-start | bytes 786440 | tf_op jit(solution)/shard_map/ppermute | solution.py:364
  130.4 0.1 collective-permute-done.23.got
  130.6 0.1 collective-permute-start.24
  130.7 0.2 collective-permute-done.16.g1
  130.8 6.6 %collective-permute-done.17.g2 = bf16[256,512]{1,0:T(8,128)(2,1)S(1)} collective-permute-done((bf16[256,512]{1,0:T(8,128)(2,1)}, bf16[256,512]{1,0:T(8,128)(2,1)S(1)}, u32[]{:S(2)}, u32[]{:S(2)}) %collective-permute-start.17) | collective-permute-done | bytes 262176 | tf_op jit(solution)/shard_map/ppermute | solution.py:364
  137.4 2.0 %collective-permute-done.18.g3 = bf16[256,512]{1,0:T(8,128)(2,1)S(1)} collective-permute-done((bf16[256,512]{1,0:T(8,128)(2,1)}, bf16[256,512]{1,0:T(8,128)(2,1)S(1)}, u32[]{:S(2)}, u32[]{:S(2)}) %collective-permute-start.18) | collective-permute-done | bytes 262176 | tf_op jit(solution)/shard_map/ppermute | solution.py:494
  139.4 1.6 %normals.1 = f32[4096,128]{1,0:T(8,128)} custom-call(f32[256,512]{1,0:T(8,128)S(1)} %copy-done.6, bf16[256,512]{1,0:T(8,128)(2,1)S(1)} %collective-permute-done.16.g1, bf16[256,512]{1,0:T(8,128)(2,1)S(1)} %collective-permute-done.17.g2, bf16[256,512]{1,0:T(8,128)(2,1)S(1)} %collective-permute-done.18.g3), custom_call_target="tpu_custom_call" | custom-call | bytes 4194304 | tf_op jit(solution)/shard_map/normals/pallas_call | solution.py:338
  141.0 1.0 chol_out.1
  (45 shorter events, 0.2 us)
Async XLA Ops:
  0.6 25.2 %copy-start = (f32[1024,512]{1,0:T(8,128)S(1)}, f32[1024,512]{1,0:T(8,128)}, u32[]{:S(2)}) copy-start(f32[1024,512]{1,0:T(8,128)} %vol_hbm.1) | copy-start | bytes 6291460
  0.6 25.2 %copy-start.3 = (f32[32,512]{1,0:T(8,128)S(1)}, f32[32,512]{1,0:T(8,128)}, u32[]{:S(2)}) copy-start(f32[32,512]{1,0:T(8,128)} %reset.5) | copy-start | bytes 196612
  0.7 25.2 %copy-start.7 = (f32[32,512]{1,0:T(8,128)S(1)}, f32[32,512]{1,0:T(8,128)}, u32[]{:S(2)}) copy-start(f32[32,512]{1,0:T(8,128)} %load.5) | copy-start | bytes 196612
  0.7 25.2 %copy-start.2 = (bf16[512,512]{1,0:T(8,128)(2,1)S(1)}, bf16[512,512]{1,0:T(8,128)(2,1)}, u32[]{:S(2)}) copy-start(bf16[512,512]{1,0:T(8,128)(2,1)} %chol.5) | copy-start | bytes 1572868
  0.7 25.2 %copy-start.8 = (s32[32]{0:T(128)S(1)}, s32[32]{0:T(128)}, u32[]{:S(2)}) copy-start(s32[32]{0:T(128)} %param.19) | copy-start | bytes 388
  0.7 25.2 %copy-start.1 = (bf16[1024,1,512]{2,0,1:T(8,128)(2,1)S(1)}, bf16[1024,1,512]{2,0,1:T(8,128)(2,1)}, u32[]{:S(2)}) copy-start(bf16[1024,1,512]{2,0,1:T(8,128)(2,1)} %param.11) | copy-start | bytes 3145732
  0.7 25.2 %copy-start.10 = (f32[32]{0:T(128)S(1)}, f32[32]{0:T(128)}, u32[]{:S(2)}) copy-start(f32[32]{0:T(128)} %param.18) | copy-start | bytes 388
  0.7 25.2 %copy-start.9 = (f32[32]{0:T(128)S(1)}, f32[32]{0:T(128)}, u32[]{:S(2)}) copy-start(f32[32]{0:T(128)} %param.17) | copy-start | bytes 388
  0.7 25.1 %collective-permute-start.1 = (bf16[64,1024]{1,0:T(8,128)(2,1)}, bf16[64,1024]{1,0:T(8,128)(2,1)}, u32[]{:S(2)}, u32[]{:S(2)}) collective-permute-start(bf16[64,1024]{1,0:T(8,128)(2,1)} %param.12), channel_id=1, source_target_pairs={{0,16},{1,17},{2,18},{3,19},{4,20},{5,21},{6,22},{7,23},{8,48},{9,... | collective-permute-start | bytes 393224 | tf_op jit(solution)/shard_map/ppermute | solution.py:396
  10.1 15.7 %collective-permute-start = (bf16[64,1024]{1,0:T(8,128)(2,1)}, bf16[64,1024]{1,0:T(8,128)(2,1)}, u32[]{:S(2)}, u32[]{:S(2)}) collective-permute-start(bf16[64,1024]{1,0:T(8,128)(2,1)} %param.12), channel_id=1, source_target_pairs={{0,0},{1,1},{2,2},{3,3},{4,4},{5,5},{6,6},{7,7},{8,32},{9,33},{10,... | collective-permute-start | bytes 393224 | tf_op jit(solution)/shard_map/ppermute | solution.py:396
  29.1 0.8 copy-start.4
  29.9 3.0 %copy-start.13 = (bf16[1024,512]{1,0:T(8,128)(2,1)S(1)}, bf16[1024,512]{1,0:T(8,128)(2,1)}, u32[]{:S(2)}) copy-start(bf16[1024,512]{1,0:T(8,128)(2,1)} %get-tuple-element.53) | copy-start | bytes 3145732
  32.7 23.5 %copy-start.5 = (f32[256,512]{1,0:T(8,128)S(1)}, f32[256,512]{1,0:T(8,128)}, u32[]{:S(2)}) copy-start(f32[256,512]{1,0:T(8,128)} %copy-done.4) | copy-start | bytes 1572868
  32.7 7.3 %collective-permute-start.7 = (f32[256,512]{1,0:T(8,128)S(1)}, f32[256,512]{1,0:T(8,128)S(1)}, u32[]{:S(2)}, u32[]{:S(2)}) collective-permute-start(f32[256,512]{1,0:T(8,128)S(1)} %get-tuple-element.49), channel_id=1, source_target_pairs={{0,64},{64,0},{1,65},{65,1},{2,66},{66,2},{3,67},{67,3},{4,68},{68... | collective-permute-start | bytes 1572872 | tf_op jit(solution)/shard_map/ppermute | solution.py:364
  33.8 15.2 %collective-permute-start.3 = (bf16[512,512]{1,0:T(8,128)(2,1)S(1)}, bf16[512,512]{1,0:T(8,128)(2,1)}, u32[]{:S(2)}, u32[]{:S(2)}) collective-permute-start(bf16[512,512]{1,0:T(8,128)(2,1)S(1)} %get-tuple-element.41), channel_id=1, source_target_pairs={{0,128},{128,0},{1,129},{129,1},{2,130},{130,2},{3,131},{131,3},{4... | collective-permute-start | bytes 1572872 | tf_op jit(solution)/shard_map/ppermute | solution.py:364
  35.3 20.9 %collective-permute-start.4 = (bf16[256,512]{1,0:T(8,128)(2,1)}, bf16[256,512]{1,0:T(8,128)(2,1)S(1)}, u32[]{:S(2)}, u32[]{:S(2)}) collective-permute-start(bf16[256,512]{1,0:T(8,128)(2,1)} %get-tuple-element.43), channel_id=1, source_target_pairs={{0,1},{1,2},{2,3},{3,0},{4,5},{5,6},{6,7},{7,4},{8,9},{9,10},{10,1... | collective-permute-start | bytes 786440 | tf_op jit(solution)/shard_map/ppermute | solution.py:368
  36.7 19.4 %collective-permute-start.5 = (bf16[256,512]{1,0:T(8,128)(2,1)}, bf16[256,512]{1,0:T(8,128)(2,1)S(1)}, u32[]{:S(2)}, u32[]{:S(2)}) collective-permute-start(bf16[256,512]{1,0:T(8,128)(2,1)} %get-tuple-element.44), channel_id=1, source_target_pairs={{0,2},{1,3},{2,0},{3,1},{4,6},{5,7},{6,4},{7,5},{8,10},{9,11},{10,... | collective-permute-start | bytes 786440 | tf_op jit(solution)/shard_map/ppermute | solution.py:368
  37.9 18.3 %collective-permute-start.6 = (bf16[256,512]{1,0:T(8,128)(2,1)S(1)}, bf16[256,512]{1,0:T(8,128)(2,1)S(1)}, u32[]{:S(2)}, u32[]{:S(2)}) collective-permute-start(bf16[256,512]{1,0:T(8,128)(2,1)S(1)} %get-tuple-element.45), channel_id=1, source_target_pairs={{0,3},{1,0},{2,1},{3,2},{4,7},{5,4},{6,5},{7,6},{8,11},{9,8},{10,9... | collective-permute-start | bytes 786440 | tf_op jit(solution)/shard_map/ppermute | solution.py:368
  40.1 16.1 %collective-permute-start.8 = (f32[128,512]{1,0:T(8,128)S(1)}, f32[128,512]{1,0:T(8,128)S(1)}, u32[]{:S(2)}, u32[]{:S(2)}) collective-permute-start(f32[128,512]{1,0:T(8,128)S(1)} %get-tuple-element.51), channel_id=1, source_target_pairs={{0,128},{128,0},{1,129},{129,1},{2,130},{130,2},{3,131},{131,3},{4... | collective-permute-start | bytes 786440 | tf_op jit(solution)/shard_map/ppermute | solution.py:364
  41.4 14.7 %all-to-all-start = ((f32[4,4,2,1024]{3,2,1,0:T(2,128)}), f32[4,4,2,1024]{3,2,1,0:T(2,128)S(1)}, u32[]{:S(2)}, u32[]{:S(2)}) async-start(f32[4,4,2,1024]{3,2,1,0:T(2,128)} %broadcast_in_dim.2), calls=%async_computation | async-start | bytes 262144 | tf_op jit(solution)/shard_map/all_to_all | solution.py:372
  49.0 14.0 %collective-permute-start.2 = (bf16[2,64,1024]{2,1,0:T(8,128)(2,1)}, bf16[2,64,1024]{2,1,0:T(8,128)(2,1)}, u32[]{:S(2)}, u32[]{:S(2)}) collective-permute-start(bf16[2,64,1024]{2,1,0:T(8,128)(2,1)} %pad_maximum_fusion.1), channel_id=1, source_target_pairs={{0,8},{8,0},{1,9},{9,1},{2,10},{10,2},{3,11},{11,3},{4,12},{12,4},... | collective-permute-start | bytes 786440 | tf_op jit(solution)/shard_map/ppermute | solution.py:364
  56.2 10.0 %copy-start.14 = (bf16[1024,512]{1,0:T(8,128)(2,1)S(1)}, bf16[1024,512]{1,0:T(8,128)(2,1)}, u32[]{:S(2)}) copy-start(bf16[1024,512]{1,0:T(8,128)(2,1)} %get-tuple-element.53) | copy-start | bytes 3145732
  57.1 19.3 %all-to-all-start.1 = ((bf16[8,48,512]{2,1,0:T(8,128)(2,1)}), bf16[8,48,512]{2,1,0:T(8,128)(2,1)S(1)}, u32[]{:S(2)}, u32[]{:S(2)}) async-start(bf16[8,48,512]{2,1,0:T(8,128)(2,1)} %sum_x.1), calls=%async_computation.1 | async-start | bytes 786432 | tf_op jit(solution)/shard_map/all_to_all | solution.py:372
  62.4 12.8 %collective-permute-start.13 = (bf16[512,512]{1,0:T(8,128)(2,1)}, bf16[512,512]{1,0:T(8,128)(2,1)S(1)}, u32[]{:S(2)}, u32[]{:S(2)}) collective-permute-start(bf16[512,512]{1,0:T(8,128)(2,1)} %get-tuple-element.54), channel_id=1, source_target_pairs={{0,128},{128,0},{1,129},{129,1},{2,130},{130,2},{3,131},{131,3},{4... | collective-permute-start | bytes 1572872 | tf_op jit(solution)/shard_map/ppermute | solution.py:364
  64.1 42.1 %copy-start.15 = (bf16[4,64,1024]{2,1,0:T(8,128)(2,1)}, bf16[4,64,1024]{2,1,0:T(8,128)(2,1)S(1)}, u32[]{:S(2)}) copy-start(bf16[4,64,1024]{2,1,0:T(8,128)(2,1)S(1)} %pad_maximum_fusion.b0) | copy-start | bytes 1572868
  64.1 14.8 %collective-permute-start.11 = (bf16[4,64,1024]{2,1,0:T(8,128)(2,1)S(1)}, bf16[4,64,1024]{2,1,0:T(8,128)(2,1)}, u32[]{:S(2)}, u32[]{:S(2)}) collective-permute-start(bf16[4,64,1024]{2,1,0:T(8,128)(2,1)S(1)} %pad_maximum_fusion.b0), channel_id=1, source_target_pairs={{0,3},{1,0},{2,1},{3,2},{4,7},{5,4},{6,5},{7,6},{8,11},{9,8},{10,9... | collective-permute-start | bytes 1572872 | tf_op jit(solution)/shard_map/ppermute | solution.py:368
  64.4 14.9 %collective-permute-start.9 = (bf16[4,64,1024]{2,1,0:T(8,128)(2,1)S(1)}, bf16[4,64,1024]{2,1,0:T(8,128)(2,1)}, u32[]{:S(2)}, u32[]{:S(2)}) collective-permute-start(bf16[4,64,1024]{2,1,0:T(8,128)(2,1)S(1)} %pad_maximum_fusion.b0), channel_id=1, source_target_pairs={{0,1},{1,2},{2,3},{3,0},{4,5},{5,6},{6,7},{7,4},{8,9},{9,10},{10,1... | collective-permute-start | bytes 1572872 | tf_op jit(solution)/shard_map/ppermute | solution.py:368
  66.2 40.0 %collective-permute-start.12 = (bf16[1024,512]{1,0:T(8,128)(2,1)S(1)}, bf16[1024,512]{1,0:T(8,128)(2,1)}, u32[]{:S(2)}, u32[]{:S(2)}) collective-permute-start(bf16[1024,512]{1,0:T(8,128)(2,1)S(1)} %copy-done.14), channel_id=1, source_target_pairs={{0,64},{64,0},{1,65},{65,1},{2,66},{66,2},{3,67},{67,3},{4,68},{68... | collective-permute-start | bytes 3145736 | tf_op jit(solution)/shard_map/ppermute | solution.py:364
  67.7 1.3 copy-start.11
  69.1 37.2 %copy-start.12 = (f32[4,32,512]{2,1,0:T(8,128)}, f32[4,32,512]{2,1,0:T(8,128)S(1)}, u32[]{:S(2)}) copy-start(f32[4,32,512]{2,1,0:T(8,128)S(1)} %get-tuple-element.56.radj) | copy-start | bytes 786436
  75.3 31.0 %copy-start.16 = (bf16[512,512]{1,0:T(8,128)(2,1)}, bf16[512,512]{1,0:T(8,128)(2,1)S(1)}, u32[]{:S(2)}) copy-start(bf16[512,512]{1,0:T(8,128)(2,1)S(1)} %collective-permute-done.13.s2b) | copy-start | bytes 1572868
  76.4 6.4 %collective-permute-start.19 = (f32[48,512]{1,0:T(8,128)S(1)}, f32[48,512]{1,0:T(8,128)S(1)}, u32[]{:S(2)}, u32[]{:S(2)}) collective-permute-start(f32[48,512]{1,0:T(8,128)S(1)} %sum_z.1.own), channel_id=1, source_target_pairs={{0,32},{32,0},{1,33},{33,1},{2,34},{34,2},{3,35},{35,3},{4,36},{36... | collective-permute-start | bytes 294920 | tf_op jit(solution)/shard_map/ppermute | solution.py:364
  83.6 18.4 %all-to-all-start.2 = ((bf16[8,48,512]{2,1,0:T(8,128)(2,1)}), bf16[8,48,512]{2,1,0:T(8,128)(2,1)S(1)}, u32[]{:S(2)}, u32[]{:S(2)}) async-start(bf16[8,48,512]{2,1,0:T(8,128)(2,1)} %totals.1), calls=%async_computation.2 | async-start | bytes 786432 | tf_op jit(solution)/shard_map/all_to_all | solution.py:372
  89.4 12.5 %collective-permute-start.10 = (bf16[4,64,1024]{2,1,0:T(8,128)(2,1)S(1)}, bf16[4,64,1024]{2,1,0:T(8,128)(2,1)}, u32[]{:S(2)}, u32[]{:S(2)}) collective-permute-start(bf16[4,64,1024]{2,1,0:T(8,128)(2,1)S(1)} %pad_maximum_fusion.b0), channel_id=1, source_target_pairs={{0,2},{1,3},{2,0},{3,1},{4,6},{5,7},{6,4},{7,5},{8,10},{9,11},{10,... | collective-permute-start | bytes 1572872 | tf_op jit(solution)/shard_map/ppermute | solution.py:368
  91.5 12.8 %collective-permute-start.14 = (bf16[512,512]{1,0:T(8,128)(2,1)}, bf16[512,512]{1,0:T(8,128)(2,1)}, u32[]{:S(2)}, u32[]{:S(2)}) collective-permute-start(bf16[512,512]{1,0:T(8,128)(2,1)} %collective-permute-done.3.s2a), channel_id=1, source_target_pairs={{0,64},{64,0},{1,65},{65,1},{2,66},{66,2},{3,67},{67,3},{4,68},{68... | collective-permute-start | bytes 1572872 | tf_op jit(solution)/shard_map/ppermute | solution.py:364
  91.5 14.7 %collective-permute-start.15 = (bf16[512,512]{1,0:T(8,128)(2,1)S(1)}, bf16[512,512]{1,0:T(8,128)(2,1)}, u32[]{:S(2)}, u32[]{:S(2)}) collective-permute-start(bf16[512,512]{1,0:T(8,128)(2,1)S(1)} %collective-permute-done.13.s2b), channel_id=1, source_target_pairs={{0,64},{64,0},{1,65},{65,1},{2,66},{66,2},{3,67},{67,3},{4,68},{68... | collective-permute-start | bytes 1572872 | tf_op jit(solution)/shard_map/ppermute | solution.py:364
  102.0 18.8 %collective-permute-start.22 = (bf16[384,512]{1,0:T(8,128)(2,1)S(1)}, bf16[384,512]{1,0:T(8,128)(2,1)S(1)}, u32[]{:S(2)}, u32[]{:S(2)}) collective-permute-start(bf16[384,512]{1,0:T(8,128)(2,1)S(1)} %gather_z.1.own), channel_id=1, source_target_pairs={{0,3},{1,0},{2,1},{3,2},{4,7},{5,4},{6,5},{7,6},{8,11},{9,8},{10,9... | collective-permute-start | bytes 1179656 | tf_op jit(solution)/shard_map/ppermute | solution.py:368
  103.1 17.7 %collective-permute-start.21 = (bf16[384,512]{1,0:T(8,128)(2,1)S(1)}, bf16[384,512]{1,0:T(8,128)(2,1)S(1)}, u32[]{:S(2)}, u32[]{:S(2)}) collective-permute-start(bf16[384,512]{1,0:T(8,128)(2,1)S(1)} %gather_z.1.own), channel_id=1, source_target_pairs={{0,2},{1,3},{2,0},{3,1},{4,6},{5,7},{6,4},{7,5},{8,10},{9,11},{10,... | collective-permute-start | bytes 1179656 | tf_op jit(solution)/shard_map/ppermute | solution.py:368
  104.4 16.4 %collective-permute-start.20 = (bf16[384,512]{1,0:T(8,128)(2,1)S(1)}, bf16[384,512]{1,0:T(8,128)(2,1)S(1)}, u32[]{:S(2)}, u32[]{:S(2)}) collective-permute-start(bf16[384,512]{1,0:T(8,128)(2,1)S(1)} %gather_z.1.own), channel_id=1, source_target_pairs={{0,1},{1,2},{2,3},{3,0},{4,5},{5,6},{6,7},{7,4},{8,9},{9,10},{10,1... | collective-permute-start | bytes 1179656 | tf_op jit(solution)/shard_map/ppermute | solution.py:368
  120.8 18.6 %copy-start.6 = (f32[256,512]{1,0:T(8,128)S(1)}, f32[256,512]{1,0:T(8,128)}, u32[]{:S(2)}) copy-start(f32[256,512]{1,0:T(8,128)} %get-tuple-element.57.own) | copy-start | bytes 1572868
  122.3 8.3 %collective-permute-start.23 = (bf16[128,512]{1,0:T(8,128)(2,1)S(1)}, bf16[128,512]{1,0:T(8,128)(2,1)S(1)}, u32[]{:S(2)}, u32[]{:S(2)}) collective-permute-start(bf16[128,512]{1,0:T(8,128)(2,1)S(1)} %get-tuple-element.66.own), channel_id=1, source_target_pairs={{0,128},{128,0},{1,129},{129,1},{2,130},{130,2},{3,131},{131,3},{4... | collective-permute-start | bytes 393224 | tf_op jit(solution)/shard_map/ppermute | solution.py:364
  124.2 6.6 %collective-permute-start.16 = (bf16[256,512]{1,0:T(8,128)(2,1)}, bf16[256,512]{1,0:T(8,128)(2,1)S(1)}, u32[]{:S(2)}, u32[]{:S(2)}) collective-permute-start(bf16[256,512]{1,0:T(8,128)(2,1)} %get-tuple-element.58), channel_id=1, source_target_pairs={{0,4},{4,0},{1,5},{5,1},{2,6},{6,2},{3,7},{7,3},{8,12},{12,8},{9,1... | collective-permute-start | bytes 786440 | tf_op jit(solution)/shard_map/ppermute | solution.py:364
  126.3 11.1 %collective-permute-start.17 = (bf16[256,512]{1,0:T(8,128)(2,1)}, bf16[256,512]{1,0:T(8,128)(2,1)S(1)}, u32[]{:S(2)}, u32[]{:S(2)}) collective-permute-start(bf16[256,512]{1,0:T(8,128)(2,1)} %get-tuple-element.59), channel_id=1, source_target_pairs={{0,32},{32,0},{1,33},{33,1},{2,34},{34,2},{3,35},{35,3},{4,36},{36... | collective-permute-start | bytes 786440 | tf_op jit(solution)/shard_map/ppermute | solution.py:364
  130.4 9.0 %collective-permute-start.18 = (bf16[256,512]{1,0:T(8,128)(2,1)}, bf16[256,512]{1,0:T(8,128)(2,1)S(1)}, u32[]{:S(2)}, u32[]{:S(2)}) collective-permute-start(bf16[256,512]{1,0:T(8,128)(2,1)} %get-tuple-element.60), channel_id=1, source_target_pairs={{0,36},{4,32},{32,4},{36,0},{1,37},{5,33},{33,5},{37,1},{2,38},{6,... | collective-permute-start | bytes 786440 | tf_op jit(solution)/shard_map/ppermute | solution.py:494
  130.6 10.4 %collective-permute-start.24 = (bf16[256,512]{1,0:T(8,128)(2,1)S(1)}, bf16[256,512]{1,0:T(8,128)(2,1)S(1)}, u32[]{:S(2)}, u32[]{:S(2)}) collective-permute-start(bf16[256,512]{1,0:T(8,128)(2,1)S(1)} %chol_half.1.own), channel_id=1, source_target_pairs={{0,64},{64,0},{1,65},{65,1},{2,66},{66,2},{3,67},{67,3},{4,68},{68... | collective-permute-start | bytes 786440 | tf_op jit(solution)/shard_map/ppermute | solution.py:364
